TPU v7x, 128 devices: a whole 4x4x4 slice. The times are simulated.
128 devices in a mesh: floor: 16 (over z, x), slab: 8 (over y, core).
Axes of the slice: x: 4, y: 4, z: 4, core: 2. Of those that a mesh axis runs over, the one named last changes fastest.
Arguments:
- latent: bfloat16 [8, 65536, 128], P('slab', 'floor'), may hold values from -6 to 6
- edge_geom: float32 [8, 3, 1048576], P('slab', None, 'floor'), may hold values from -3 to 3
- edge_recv: int32 [8, 1048576], P('slab', 'floor'), may hold values from 0 to 4095, as said below
- edge_send: int32 [8, 1048576], P('slab', 'floor'), may hold values from 0 to 9215, as said below
- ghost_rows: int32 [8, 160, 512], P('slab', 'floor'), may hold values from 0 to 4095
- dest: int32 [8, 65536], P('slab', 'floor'), may hold values from 0 to 15, as said below
- enc_w1: float32 [4, 128], replicated, may hold values from -3 to 3
- enc_b1: float32 [128], replicated, may hold values from -3 to 3
- enc_w2: bfloat16 [128, 128], replicated, may hold values from -0.5 to 0.5
- pe_w1: bfloat16 [3, 128, 128], replicated, may hold values from -0.3125 to 0.3125
- pe_w2: bfloat16 [128, 128], replicated, may hold values from -0.5 to 0.5
- edge_gain: float32 [128], replicated, may hold values from 0.5 to 1.5
- pn_w1: bfloat16 [2, 128, 128], replicated, may hold values from -0.375 to 0.375
- pn_w2: bfloat16 [128, 128], replicated, may hold values from -0.5 to 0.5
- node_gain: float32 [128], replicated, may hold values from 0.5 to 1.5
Outputs:
- staying: bfloat16 [8, 65536, 128], P('slab', 'floor')
- arrivals: bfloat16 [8, 128, 128, 128], P('slab', 'floor')
Inputs may be any that keep to these rules, and one draw needn't show every extreme that they name: A particle's dest is its own brick or one of the bricks one step away in the floor grid (rows and columns each differ by at most 1). At most 128 rows of one brick in one slab have dest equal to any one other brick. `edge_send`: A value v < 4096 names row v of the own brick; v = 4096 + k * 512 + j names slot j of ghost block k of ext. Blocks whose source brick or slab lies outside the grid are never named. `edge_recv`: A brick's edges come in tiles of 2048 entries: every entry of tile t names a row from t * 128 to (t + 1) * 128 - 1 of the own brick.
All inputs are finite; a program needn't handle non-finite values.
Results may differ from a plain program's by a relative error of at most 0.0054.
Values may be sent and summed in bfloat16 or wider, within the bound.
A program may use at most 128 MiB of HBM per device.

v0:
```python
import math

import jax
import jax.numpy as jnp
from jax import lax
from jax.sharding import PartitionSpec as P

BCOLS = 4
NEIGH = 16
MCAP = 128


STEP_ROW = (-1, -1, -1, 0, 0, 1, 1, 1)
STEP_COL = (-1, 0, 1, -1, 1, -1, 0, 1)
norm_eps = 1e-05


def from_behind(value, axis, steps):
    count = lax.axis_size(axis)
    first, last = (max(0, -steps), min(count, count - steps))
    return lax.ppermute(value, axis, [(source, source + steps) for source in range(first, last)])


def extended_2(block, sides, width):
    for axis, dim in sides:
        count = lax.axis_size(axis)
        forward = [(i, i + 1) for i in range(count - 1)]
        backward = [(target, source) for source, target in forward]
        low = lax.ppermute(
            lax.slice_in_dim(block, block.shape[dim] - width, None, axis=dim), axis, forward
        )
        high = lax.ppermute(lax.slice_in_dim(block, 0, width, axis=dim), axis, backward)
        block = jnp.concatenate([low, block, high], axis=dim)
    return block


def layer_norm(values):
    centred = values - jnp.mean(values, axis=-1, keepdims=True)
    spread = jnp.mean(centred * centred, axis=-1, keepdims=True)
    return centred / jnp.sqrt(spread + norm_eps)


def floor_ghosts(blocks):
    return jnp.stack(
        [
            from_behind(
                blocks[direction], "floor", STEP_ROW[direction] * BCOLS + STEP_COL[direction]
            )
            for direction in range(8)
        ]
    )


def floor_migrants(blocks):
    return jnp.stack(
        [
            from_behind(
                blocks[direction], "floor", STEP_ROW[direction] * BCOLS + STEP_COL[direction]
            )
            for direction in range(8)
        ]
    )


def per_device(
    latent,
    edge_geom,
    edge_recv,
    edge_send,
    ghost_rows,
    dest,
    enc_w1,
    enc_b1,
    enc_w2,
    pe_w1,
    pe_w2,
    edge_gain,
    pn_w1,
    pn_w2,
    node_gain,
):
    own = latent[0]
    part_dev, width = own.shape
    ghost_cap = ghost_rows.shape[2]
    brick = lax.axis_index("floor")
    packets = jnp.take(own, ghost_rows[0].reshape(-1), axis=0).reshape(10, ghost_cap, width)
    floor_blocks = floor_ghosts(packets[:8])
    vertical = extended_2(packets[8:], (("slab", 0),), 1)
    extended = jnp.concatenate(
        [own, floor_blocks.reshape(8 * ghost_cap, width), vertical[3], vertical[0]], axis=0
    )
    recv_proj = jnp.dot(own, pe_w1[1], preferred_element_type=jnp.float32).astype(jnp.bfloat16)
    send_proj = jnp.dot(extended, pe_w1[2], preferred_element_type=jnp.float32).astype(jnp.bfloat16)
    geom_all = edge_geom[0]
    receivers_all = edge_recv[0]
    senders_all = edge_send[0]
    row_tile = min(128, part_dev)
    tile_edges = row_tile * NEIGH
    tile_count = part_dev // row_tile
    group = math.gcd(tile_count, 8)
    group_edges = group * tile_edges
    group_rows = group * row_tile
    columns = jnp.arange(row_tile, dtype=jnp.int32)

    def edge_group(index):
        start = index * group_edges
        geom = lax.dynamic_slice_in_dim(geom_all, start, group_edges, 1)
        receivers = lax.dynamic_slice_in_dim(receivers_all, start, group_edges, 0)
        senders = lax.dynamic_slice_in_dim(senders_all, start, group_edges, 0)
        bases = (index * group + jnp.arange(group, dtype=jnp.int32)) * row_tile
        local = receivers.reshape(group, tile_edges) - bases[:, None]
        picks = local[:, :, None] == columns[None, None, :]
        tile_proj = lax.dynamic_slice_in_dim(recv_proj, index * group_rows, group_rows, 0).reshape(
            group, row_tile, width
        )
        recv_terms = jnp.einsum(
            "get,gtd->ged",
            picks.astype(jnp.bfloat16),
            tile_proj,
            preferred_element_type=jnp.float32,
        ).reshape(group_edges, width)
        length = jnp.sqrt(geom[0] * geom[0] + geom[1] * geom[1] + geom[2] * geom[2])
        first = (
            enc_b1[None, :]
            + geom[0][:, None] * enc_w1[0][None, :]
            + geom[1][:, None] * enc_w1[1][None, :]
            + geom[2][:, None] * enc_w1[2][None, :]
            + length[:, None] * enc_w1[3][None, :]
        )
        enc_hidden = jax.nn.relu(first).astype(jnp.bfloat16)
        encoded = layer_norm(jnp.dot(enc_hidden, enc_w2, preferred_element_type=jnp.float32))
        encoded_half = encoded.astype(jnp.bfloat16)
        before = (
            jnp.dot(encoded_half, pe_w1[0], preferred_element_type=jnp.float32)
            + recv_terms
            + jnp.take(send_proj, senders, axis=0).astype(jnp.float32)
        )
        edge_hidden = jax.nn.relu(before).astype(jnp.bfloat16)
        message = encoded + edge_gain * layer_norm(
            jnp.dot(edge_hidden, pe_w2, preferred_element_type=jnp.float32)
        )
        summed = jnp.einsum(
            "get,ged->gtd",
            picks.astype(jnp.float32),
            message.reshape(group, tile_edges, width),
            precision=lax.Precision.HIGHEST,
            preferred_element_type=jnp.float32,
        )
        return summed.reshape(group_rows, width)

    aggregate = lax.map(edge_group, jnp.arange(tile_count // group, dtype=jnp.int32)).reshape(
        part_dev, width
    )
    node_pre = jnp.dot(own, pn_w1[0], preferred_element_type=jnp.float32) + jnp.dot(
        aggregate.astype(jnp.bfloat16), pn_w1[1], preferred_element_type=jnp.float32
    )
    node_hidden = jax.nn.relu(node_pre).astype(jnp.bfloat16)
    updated = (
        own.astype(jnp.float32)
        + node_gain * layer_norm(jnp.dot(node_hidden, pn_w2, preferred_element_type=jnp.float32))
    ).astype(jnp.bfloat16)
    targets = dest[0]
    staying = jnp.where((targets == brick)[:, None], updated, jnp.zeros_like(updated))
    move_row = targets // BCOLS - brick // BCOLS
    move_col = targets % BCOLS - brick % BCOLS
    move_code = (move_row + 1) * 3 + move_col + 1
    heading = jnp.where(move_code > 4, move_code - 1, move_code)
    moving = move_code != 4
    onehot = (heading[:, None] == jnp.arange(8, dtype=jnp.int32)[None, :]) & moving[:, None]
    running = jnp.cumsum(onehot.astype(jnp.int32), axis=0)
    rank = jnp.sum(jnp.where(onehot, running, 0), axis=1) - 1
    slot = jnp.where(moving, heading * MCAP + rank, 8 * MCAP)
    outgoing = jnp.zeros((8 * MCAP, width), jnp.bfloat16).at[slot].set(updated, mode="drop")
    arrived = floor_migrants(outgoing.reshape(8, MCAP, width))
    return (staying[None], arrived[None])


def solution(mesh):
    in_specs = (
        P("slab", "floor", None),
        P("slab", None, "floor"),
        P("slab", "floor"),
        P("slab", "floor"),
        P("slab", "floor", None),
        P("slab", "floor"),
        P(),
        P(),
        P(),
        P(),
        P(),
        P(),
        P(),
        P(),
        P(),
    )
    out_specs = (P("slab", "floor", None), P("slab", "floor", None, None))
    return jax.shard_map(
        per_device, mesh=mesh, in_specs=in_specs, out_specs=out_specs, check_vma=False
    )
```

profile of v0, /device:TPU:1, one launch (start us, length us, event | category | flops | bytes accessed | tf_op | source)
XLA Modules:
  0.0 666.1 jit_solution(5568736835552034498)
XLA Ops:
  2.2 19.3 %gather_fusion.1 = bf16[5120,128]{1,0:T(8,128)(2,1)} fusion(bf16[4096,128]{1,0:T(8,128)(2,1)} %bitcast.177, s32[5120]{0:T(1024)S(1)} %broadcast_clamp_fusion), kind=kCustom, calls=%fused_computation.1 | custom fusion | bytes 2641920 | tf_op jit(solution)/shard_map/jit(_take)/gather | solution.py:86
  59.4 7.2 %collective-permute-done.2 = bf16[512,128]{0,1:T(8,128)(2,1)S(1)} collective-permute-done((bf16[512,128]{0,1:T(8,128)(2,1)}, bf16[512,128]{0,1:T(8,128)(2,1)S(1)}, u32[]{:S(2)}, u32[]{:S(2)}) %collective-permute-start.2) | collective-permute-done | bytes 131104 | tf_op jit(solution)/shard_map/ppermute | solution.py:21
  93.8 517.6 %while.11 = (s32[]{:T(128)}, bf16[4,1024,128]{2,1,0:T(8,128)(2,1)}, s32[4]{0:T(128)S(1)}, s32[65536]{0:T(1024)}, f32[128]{0:T(128)S(1)}, /*index=5*/f32[3,65536]...) while((s32[]{:T(128)}, bf16[4,1024,128]{2,1,0:T(8,128)(2,1)}, ...), condition=%wide.region_5.6_spmd.clone, body=%wide.region_0.5_spmd.clone.sunk | while | flops 5442404352 | bytes 176954928 | solution.py:151
  101.8 57.8 %gather_fusion = bf16[16384,128]{1,0:T(8,128)(2,1)} fusion(bf16[9216,128]{1,0:T(8,128)(2,1)S(1)} %get-tuple-element.345, s32[16384]{0:T(1024)S(1)} %fusion.125), kind=kCustom, calls=%fused_computation.clone.clone.1 | custom fusion | bytes 8454144 | tf_op jit(solution)/shard_map/while/body/eval_jaxpr/jit(_take)/gather | solution.py:136
  165.3 11.3 %fusion.126 = (f32[16384]{0:T(1024)S(1)}, f32[16384,128]{1,0:T(8,128)S(1)}) fusion(bf16[128,128]{1,0:T(8,128)(2,1)S(1)} %copy-done.16, f32[128]{0:T(128)S(1)} %get-tuple-element.276, f32[16384]{0:T(1024)S(1)} %add_sqrt_fusion.7, f32[128]{0:T(128)S(1)} %get-tuple-element.280, f32[16384]{0:T(1024)S(1)} %bitcast.185, f32[128]{0:T(128)S(1)} %get-tuple-element.281, ...), kind=kOutput, calls=%fused_computation.171.clone.1 | convolution fusion | flops 559923200 | bytes 8751616 | tf_op jit(solution)/shard_map/while/body/eval_jaxpr/dot_general | solution.py:131
  184.6 14.0 %fusion.127 = (f32[16384]{0:T(1024)S(1)}, f32[16384,128]{1,0:T(8,128)}) fusion(bf16[128,128]{1,0:T(8,128)(2,1)S(1)} %copy-done.17, f32[16384,128]{1,0:T(8,128)} %bitcast.176, bf16[16384,128]{1,0:T(8,128)(2,1)} %gather_fusion, pred[16384]{0:T(1024)(128)(4,1)S(1)} %compare_and_fusion.3, bf16[3,128,128]{2,1,0:T(8,128)(2,1)S(1)} %get-tuple-element.342, ...), kind=kOutput, calls=%fused_computation.172.clone.1 | convolution fusion | flops 1094696960 | bytes 29638656 | tf_op jit(solution)/shard_map/while/body/eval_jaxpr/dot_general | solution.py:140
  198.6 7.3 %multiply_reduce_fusion.6 = f32[16384]{0:T(1024)S(1)} fusion(f32[16384,128]{1,0:T(8,128)} %get-tuple-element.285, f32[16384]{0:T(1024)S(1)} %broadcast_multiply_fusion.6), kind=kLoop, calls=%fused_computation.12.clone.1 | loop fusion | flops 6275072 | bytes 8519680 | tf_op jit(solution)/shard_map/while/body/eval_jaxpr/reduce_sum | solution.py:39
  205.9 11.1 %multiply_add_fusion.2 = f32[16384,128]{1,0:T(8,128)S(1)} fusion(f32[16384,128]{1,0:T(8,128)} %get-tuple-element.285, f32[16384]{0:T(1024)S(1)} %add_sqrt_fusion.9, f32[16384]{0:T(1024)S(1)} %broadcast_multiply_fusion.6, f32[128]{0:T(128)S(1)} %get-tuple-element.341, f32[16384]{0:T(1024)S(1)} %add_sqrt_fusion.8, f32[16384,128]{1,0:T(8,128)S(1)} %copy-done.2, ...), kind=kLoop, calls=%fused_computation.11.clone.1 | loop fusion | flops 12582912 | bytes 25428480 | tf_op jit(solution)/shard_map/while/body/eval_jaxpr/add | solution.py:139
  231.1 57.8 %gather_fusion = bf16[16384,128]{1,0:T(8,128)(2,1)} fusion(bf16[9216,128]{1,0:T(8,128)(2,1)S(1)} %get-tuple-element.345, s32[16384]{0:T(1024)S(1)} %fusion.125), kind=kCustom, calls=%fused_computation.clone.clone.1 | custom fusion | bytes 8454144 | tf_op jit(solution)/shard_map/while/body/eval_jaxpr/jit(_take)/gather | solution.py:136
  294.5 11.3 %fusion.126 = (f32[16384]{0:T(1024)S(1)}, f32[16384,128]{1,0:T(8,128)S(1)}) fusion(bf16[128,128]{1,0:T(8,128)(2,1)S(1)} %copy-done.16, f32[128]{0:T(128)S(1)} %get-tuple-element.276, f32[16384]{0:T(1024)S(1)} %add_sqrt_fusion.7, f32[128]{0:T(128)S(1)} %get-tuple-element.280, f32[16384]{0:T(1024)S(1)} %bitcast.185, f32[128]{0:T(128)S(1)} %get-tuple-element.281, ...), kind=kOutput, calls=%fused_computation.171.clone.1 | convolution fusion | flops 559923200 | bytes 8751616 | tf_op jit(solution)/shard_map/while/body/eval_jaxpr/dot_general | solution.py:131
  313.9 14.0 %fusion.127 = (f32[16384]{0:T(1024)S(1)}, f32[16384,128]{1,0:T(8,128)}) fusion(bf16[128,128]{1,0:T(8,128)(2,1)S(1)} %copy-done.17, f32[16384,128]{1,0:T(8,128)} %bitcast.176, bf16[16384,128]{1,0:T(8,128)(2,1)} %gather_fusion, pred[16384]{0:T(1024)(128)(4,1)S(1)} %compare_and_fusion.3, bf16[3,128,128]{2,1,0:T(8,128)(2,1)S(1)} %get-tuple-element.342, ...), kind=kOutput, calls=%fused_computation.172.clone.1 | convolution fusion | flops 1094696960 | bytes 29638656 | tf_op jit(solution)/shard_map/while/body/eval_jaxpr/dot_general | solution.py:140
  327.8 7.3 %multiply_reduce_fusion.6 = f32[16384]{0:T(1024)S(1)} fusion(f32[16384,128]{1,0:T(8,128)} %get-tuple-element.285, f32[16384]{0:T(1024)S(1)} %broadcast_multiply_fusion.6), kind=kLoop, calls=%fused_computation.12.clone.1 | loop fusion | flops 6275072 | bytes 8519680 | tf_op jit(solution)/shard_map/while/body/eval_jaxpr/reduce_sum | solution.py:39
  335.2 11.1 %multiply_add_fusion.2 = f32[16384,128]{1,0:T(8,128)S(1)} fusion(f32[16384,128]{1,0:T(8,128)} %get-tuple-element.285, f32[16384]{0:T(1024)S(1)} %add_sqrt_fusion.9, f32[16384]{0:T(1024)S(1)} %broadcast_multiply_fusion.6, f32[128]{0:T(128)S(1)} %get-tuple-element.341, f32[16384]{0:T(1024)S(1)} %add_sqrt_fusion.8, f32[16384,128]{1,0:T(8,128)S(1)} %copy-done.2, ...), kind=kLoop, calls=%fused_computation.11.clone.1 | loop fusion | flops 12582912 | bytes 25428480 | tf_op jit(solution)/shard_map/while/body/eval_jaxpr/add | solution.py:139
  360.5 57.8 %gather_fusion = bf16[16384,128]{1,0:T(8,128)(2,1)} fusion(bf16[9216,128]{1,0:T(8,128)(2,1)S(1)} %get-tuple-element.345, s32[16384]{0:T(1024)S(1)} %fusion.125), kind=kCustom, calls=%fused_computation.clone.clone.1 | custom fusion | bytes 8454144 | tf_op jit(solution)/shard_map/while/body/eval_jaxpr/jit(_take)/gather | solution.py:136
  424.0 11.3 %fusion.126 = (f32[16384]{0:T(1024)S(1)}, f32[16384,128]{1,0:T(8,128)S(1)}) fusion(bf16[128,128]{1,0:T(8,128)(2,1)S(1)} %copy-done.16, f32[128]{0:T(128)S(1)} %get-tuple-element.276, f32[16384]{0:T(1024)S(1)} %add_sqrt_fusion.7, f32[128]{0:T(128)S(1)} %get-tuple-element.280, f32[16384]{0:T(1024)S(1)} %bitcast.185, f32[128]{0:T(128)S(1)} %get-tuple-element.281, ...), kind=kOutput, calls=%fused_computation.171.clone.1 | convolution fusion | flops 559923200 | bytes 8751616 | tf_op jit(solution)/shard_map/while/body/eval_jaxpr/dot_general | solution.py:131
  443.3 14.0 %fusion.127 = (f32[16384]{0:T(1024)S(1)}, f32[16384,128]{1,0:T(8,128)}) fusion(bf16[128,128]{1,0:T(8,128)(2,1)S(1)} %copy-done.17, f32[16384,128]{1,0:T(8,128)} %bitcast.176, bf16[16384,128]{1,0:T(8,128)(2,1)} %gather_fusion, pred[16384]{0:T(1024)(128)(4,1)S(1)} %compare_and_fusion.3, bf16[3,128,128]{2,1,0:T(8,128)(2,1)S(1)} %get-tuple-element.342, ...), kind=kOutput, calls=%fused_computation.172.clone.1 | convolution fusion | flops 1094696960 | bytes 29638656 | tf_op jit(solution)/shard_map/while/body/eval_jaxpr/dot_general | solution.py:140
  457.3 7.3 %multiply_reduce_fusion.6 = f32[16384]{0:T(1024)S(1)} fusion(f32[16384,128]{1,0:T(8,128)} %get-tuple-element.285, f32[16384]{0:T(1024)S(1)} %broadcast_multiply_fusion.6), kind=kLoop, calls=%fused_computation.12.clone.1 | loop fusion | flops 6275072 | bytes 8519680 | tf_op jit(solution)/shard_map/while/body/eval_jaxpr/reduce_sum | solution.py:39
  464.6 11.1 %multiply_add_fusion.2 = f32[16384,128]{1,0:T(8,128)S(1)} fusion(f32[16384,128]{1,0:T(8,128)} %get-tuple-element.285, f32[16384]{0:T(1024)S(1)} %add_sqrt_fusion.9, f32[16384]{0:T(1024)S(1)} %broadcast_multiply_fusion.6, f32[128]{0:T(128)S(1)} %get-tuple-element.341, f32[16384]{0:T(1024)S(1)} %add_sqrt_fusion.8, f32[16384,128]{1,0:T(8,128)S(1)} %copy-done.2, ...), kind=kLoop, calls=%fused_computation.11.clone.1 | loop fusion | flops 12582912 | bytes 25428480 | tf_op jit(solution)/shard_map/while/body/eval_jaxpr/add | solution.py:139
  489.8 57.8 %gather_fusion = bf16[16384,128]{1,0:T(8,128)(2,1)} fusion(bf16[9216,128]{1,0:T(8,128)(2,1)S(1)} %get-tuple-element.345, s32[16384]{0:T(1024)S(1)} %fusion.125), kind=kCustom, calls=%fused_computation.clone.clone.1 | custom fusion | bytes 8454144 | tf_op jit(solution)/shard_map/while/body/eval_jaxpr/jit(_take)/gather | solution.py:136
  553.2 11.3 %fusion.126 = (f32[16384]{0:T(1024)S(1)}, f32[16384,128]{1,0:T(8,128)S(1)}) fusion(bf16[128,128]{1,0:T(8,128)(2,1)S(1)} %copy-done.16, f32[128]{0:T(128)S(1)} %get-tuple-element.276, f32[16384]{0:T(1024)S(1)} %add_sqrt_fusion.7, f32[128]{0:T(128)S(1)} %get-tuple-element.280, f32[16384]{0:T(1024)S(1)} %bitcast.185, f32[128]{0:T(128)S(1)} %get-tuple-element.281, ...), kind=kOutput, calls=%fused_computation.171.clone.1 | convolution fusion | flops 559923200 | bytes 8751616 | tf_op jit(solution)/shard_map/while/body/eval_jaxpr/dot_general | solution.py:131
  572.5 14.0 %fusion.127 = (f32[16384]{0:T(1024)S(1)}, f32[16384,128]{1,0:T(8,128)}) fusion(bf16[128,128]{1,0:T(8,128)(2,1)S(1)} %copy-done.17, f32[16384,128]{1,0:T(8,128)} %bitcast.176, bf16[16384,128]{1,0:T(8,128)(2,1)} %gather_fusion, pred[16384]{0:T(1024)(128)(4,1)S(1)} %compare_and_fusion.3, bf16[3,128,128]{2,1,0:T(8,128)(2,1)S(1)} %get-tuple-element.342, ...), kind=kOutput, calls=%fused_computation.172.clone.1 | convolution fusion | flops 1094696960 | bytes 29638656 | tf_op jit(solution)/shard_map/while/body/eval_jaxpr/dot_general | solution.py:140
  586.5 7.3 %multiply_reduce_fusion.6 = f32[16384]{0:T(1024)S(1)} fusion(f32[16384,128]{1,0:T(8,128)} %get-tuple-element.285, f32[16384]{0:T(1024)S(1)} %broadcast_multiply_fusion.6), kind=kLoop, calls=%fused_computation.12.clone.1 | loop fusion | flops 6275072 | bytes 8519680 | tf_op jit(solution)/shard_map/while/body/eval_jaxpr/reduce_sum | solution.py:39
  593.9 11.1 %multiply_add_fusion.2 = f32[16384,128]{1,0:T(8,128)S(1)} fusion(f32[16384,128]{1,0:T(8,128)} %get-tuple-element.285, f32[16384]{0:T(1024)S(1)} %add_sqrt_fusion.9, f32[16384]{0:T(1024)S(1)} %broadcast_multiply_fusion.6, f32[128]{0:T(128)S(1)} %get-tuple-element.341, f32[16384]{0:T(1024)S(1)} %add_sqrt_fusion.8, f32[16384,128]{1,0:T(8,128)S(1)} %copy-done.2, ...), kind=kLoop, calls=%fused_computation.11.clone.1 | loop fusion | flops 12582912 | bytes 25428480 | tf_op jit(solution)/shard_map/while/body/eval_jaxpr/add | solution.py:139
  618.1 10.9 %scatter_custom_fusion = bf16[1024,128]{1,0:T(8,128)(2,1)S(1)} fusion(s32[4096]{0:T(1024)} %bitcast.199, bf16[4096,128]{1,0:T(8,128)(2,1)S(1)} %copy.28, bf16[]{:T(256)} %constant.137.clone.1), kind=kCustom, calls=%fused_computation.90 | custom fusion | bytes 262656 | tf_op jit(solution)/shard_map/scatter | solution.py:173
  (224 shorter events, 212.8 us)
Async XLA Ops:
  0.6 610.7 %copy-start = (bf16[128,128]{1,0:T(8,128)(2,1)S(1)}, bf16[128,128]{1,0:T(8,128)(2,1)}, u32[]{:S(2)}) copy-start(bf16[128,128]{1,0:T(8,128)(2,1)} %param.30) | copy-start | bytes 98308
  21.4 24.9 %copy-start.8 = (bf16[2,128,128]{2,1,0:T(8,128)(2,1)S(1)}, bf16[2,128,128]{2,1,0:T(8,128)(2,1)}, u32[]{:S(2)}) copy-start(bf16[2,128,128]{2,1,0:T(8,128)(2,1)} %param.29) | copy-start | bytes 196612
  23.1 25.0 %copy-start.13 = (bf16[3,128,128]{2,1,0:T(8,128)(2,1)S(1)}, bf16[3,128,128]{2,1,0:T(8,128)(2,1)}, u32[]{:S(2)}) copy-start(bf16[3,128,128]{2,1,0:T(8,128)(2,1)} %param.26) | copy-start | bytes 294916
  24.3 25.9 %copy-start.6 = (f32[1,3,65536]{2,0,1:T(1,128)S(1)}, f32[1,3,65536]{2,0,1:T(1,128)}, u32[]{:S(2)}) copy-start(f32[1,3,65536]{2,0,1:T(1,128)} %param.18) | copy-start | bytes 2359300
  24.3 64.3 %collective-permute-start.7 = (bf16[512,128]{0,1:T(8,128)(2,1)}, bf16[512,128]{0,1:T(8,128)(2,1)}, u32[]{:S(2)}, u32[]{:S(2)}) collective-permute-start(bf16[512,128]{0,1:T(8,128)(2,1)} %get-tuple-element.159), channel_id=1, source_target_pairs={{0,40},{8,48},{16,56},{24,64},{32,72},{40,80},{48,88},{56,96},{64,... | collective-permute-start | bytes 393224 | tf_op jit(solution)/shard_map/ppermute | solution.py:21
  30.3 61.1 %collective-permute-start.9 = (bf16[1,512,128]{1,2,0:T(8,128)(2,1)S(1)}, bf16[1,512,128]{1,2,0:T(8,128)(2,1)}, u32[]{:S(2)}, u32[]{:S(2)}) collective-permute-start(bf16[1,512,128]{1,2,0:T(8,128)(2,1)S(1)} %get-tuple-element.160), channel_id=1, source_target_pairs={{0,1},{1,2},{2,3},{3,4},{4,5},{5,6},{6,7},{8,9},{9,10},{10,11},{11... | collective-permute-start | bytes 393224 | tf_op jit(solution)/shard_map/ppermute | solution.py:29
  34.4 57.1 %collective-permute-start.8 = (bf16[1,512,128]{1,2,0:T(8,128)(2,1)S(1)}, bf16[1,512,128]{1,2,0:T(8,128)(2,1)}, u32[]{:S(2)}, u32[]{:S(2)}) collective-permute-start(bf16[1,512,128]{1,2,0:T(8,128)(2,1)S(1)} %get-tuple-element.161), channel_id=1, source_target_pairs={{1,0},{2,1},{3,2},{4,3},{5,4},{6,5},{7,6},{9,8},{10,9},{11,10},{12... | collective-permute-start | bytes 393224 | tf_op jit(solution)/shard_map/ppermute | solution.py:32
  36.3 51.3 %collective-permute-start.6 = (bf16[512,128]{0,1:T(8,128)(2,1)}, bf16[512,128]{0,1:T(8,128)(2,1)}, u32[]{:S(2)}, u32[]{:S(2)}) collective-permute-start(bf16[512,128]{0,1:T(8,128)(2,1)} %get-tuple-element.162), channel_id=1, source_target_pairs={{0,32},{8,40},{16,48},{24,56},{32,64},{40,72},{48,80},{56,88},{64,... | collective-permute-start | bytes 393224 | tf_op jit(solution)/shard_map/ppermute | solution.py:21
  40.5 11.1 %collective-permute-start = (bf16[512,128]{0,1:T(8,128)(2,1)}, bf16[512,128]{0,1:T(8,128)(2,1)}, u32[]{:S(2)}, u32[]{:S(2)}) collective-permute-start(bf16[512,128]{0,1:T(8,128)(2,1)} %get-tuple-element.168), channel_id=1, source_target_pairs={{40,0},{48,8},{56,16},{64,24},{72,32},{80,40},{88,48},{96,56},{104... | collective-permute-start | bytes 393224 | tf_op jit(solution)/shard_map/ppermute | solution.py:21
  50.1 43.6 %copy-start.4 = (bf16[1,4096,128]{1,2,0:T(8,128)(2,1)}, bf16[1,4096,128]{1,2,0:T(8,128)(2,1)S(1)}, u32[]{:S(2)}) copy-start(bf16[1,4096,128]{1,2,0:T(8,128)(2,1)S(1)} %copy.23) | copy-start | bytes 3145732
  51.7 6.4 collective-permute-start.1
  58.1 8.5 %collective-permute-start.2 = (bf16[512,128]{0,1:T(8,128)(2,1)}, bf16[512,128]{0,1:T(8,128)(2,1)S(1)}, u32[]{:S(2)}, u32[]{:S(2)}) collective-permute-start(bf16[512,128]{0,1:T(8,128)(2,1)} %get-tuple-element.166), channel_id=1, source_target_pairs={{24,0},{32,8},{40,16},{48,24},{56,32},{64,40},{72,48},{80,56},{88,... | collective-permute-start | bytes 393224 | tf_op jit(solution)/shard_map/ppermute | solution.py:21
  66.6 7.8 %collective-permute-start.3 = (bf16[512,128]{0,1:T(8,128)(2,1)}, bf16[512,128]{0,1:T(8,128)(2,1)S(1)}, u32[]{:S(2)}, u32[]{:S(2)}) collective-permute-start(bf16[512,128]{0,1:T(8,128)(2,1)} %get-tuple-element.165), channel_id=1, source_target_pairs={{8,0},{16,8},{24,16},{32,24},{40,32},{48,40},{56,48},{64,56},{72,6... | collective-permute-start | bytes 393224 | tf_op jit(solution)/shard_map/ppermute | solution.py:21
  74.5 5.3 collective-permute-start.4
  79.7 7.9 %collective-permute-start.5 = (bf16[512,128]{0,1:T(8,128)(2,1)}, bf16[512,128]{0,1:T(8,128)(2,1)S(1)}, u32[]{:S(2)}, u32[]{:S(2)}) collective-permute-start(bf16[512,128]{0,1:T(8,128)(2,1)} %get-tuple-element.163), channel_id=1, source_target_pairs={{0,24},{8,32},{16,40},{24,48},{32,56},{40,64},{48,72},{56,80},{64,... | collective-permute-start | bytes 393224 | tf_op jit(solution)/shard_map/ppermute | solution.py:21
  93.8 517.6 %copy-start.9 = (bf16[2,128,128]{2,1,0:T(8,128)(2,1)S(1)}, bf16[2,128,128]{2,1,0:T(8,128)(2,1)}, u32[]{:S(2)}) copy-start(bf16[2,128,128]{2,1,0:T(8,128)(2,1)} %param.29) | copy-start | bytes 196612
  629.1 20.4 %collective-permute-start.10 = (bf16[128,128]{1,0:T(8,128)(2,1)S(1)}, bf16[128,128]{1,0:T(8,128)(2,1)S(1)}, u32[]{:S(2)}, u32[]{:S(2)}) collective-permute-start(bf16[128,128]{1,0:T(8,128)(2,1)S(1)} %get-tuple-element.176), channel_id=1, source_target_pairs={{40,0},{48,8},{56,16},{64,24},{72,32},{80,40},{88,48},{96,56},{104... | collective-permute-start | bytes 98312 | tf_op jit(solution)/shard_map/ppermute | solution.py:21
  632.7 32.8 %collective-permute-start.17 = (bf16[128,128]{1,0:T(8,128)(2,1)S(1)}, bf16[128,128]{1,0:T(8,128)(2,1)S(1)}, u32[]{:S(2)}, u32[]{:S(2)}) collective-permute-start(bf16[128,128]{1,0:T(8,128)(2,1)S(1)} %get-tuple-element.169), channel_id=1, source_target_pairs={{0,40},{8,48},{16,56},{24,64},{32,72},{40,80},{48,88},{56,96},{64,... | collective-permute-start | bytes 98312 | tf_op jit(solution)/shard_map/ppermute | solution.py:21
  638.1 27.3 %collective-permute-start.16 = (bf16[128,128]{1,0:T(8,128)(2,1)S(1)}, bf16[128,128]{1,0:T(8,128)(2,1)S(1)}, u32[]{:S(2)}, u32[]{:S(2)}) collective-permute-start(bf16[128,128]{1,0:T(8,128)(2,1)S(1)} %get-tuple-element.170), channel_id=1, source_target_pairs={{0,32},{8,40},{16,48},{24,56},{32,64},{40,72},{48,80},{56,88},{64,... | collective-permute-start | bytes 98312 | tf_op jit(solution)/shard_map/ppermute | solution.py:21
  643.2 22.2 %collective-permute-start.15 = (bf16[128,128]{1,0:T(8,128)(2,1)S(1)}, bf16[128,128]{1,0:T(8,128)(2,1)S(1)}, u32[]{:S(2)}, u32[]{:S(2)}) collective-permute-start(bf16[128,128]{1,0:T(8,128)(2,1)S(1)} %get-tuple-element.171), channel_id=1, source_target_pairs={{0,24},{8,32},{16,40},{24,48},{32,56},{40,64},{48,72},{56,80},{64,... | collective-permute-start | bytes 98312 | tf_op jit(solution)/shard_map/ppermute | solution.py:21
  648.2 17.1 %collective-permute-start.14 = (bf16[128,128]{1,0:T(8,128)(2,1)S(1)}, bf16[128,128]{1,0:T(8,128)(2,1)S(1)}, u32[]{:S(2)}, u32[]{:S(2)}) collective-permute-start(bf16[128,128]{1,0:T(8,128)(2,1)S(1)} %get-tuple-element.172), channel_id=1, source_target_pairs={{0,8},{8,16},{16,24},{24,32},{32,40},{40,48},{48,56},{56,64},{64,7... | collective-permute-start | bytes 98312 | tf_op jit(solution)/shard_map/ppermute | solution.py:21
  649.5 4.7 collective-permute-start.11
  654.2 6.5 collective-permute-start.12
  660.7 4.6 collective-permute-start.13
  (25 other events, 159.2 us)
where the time goes:
time: 677 us; the launch traced here: 666 us
  local copies, waits for them, and re-layouts  308 us (45%)
  matrix products  154 us (23%)
  other arithmetic  108 us (16%)
  starting transfers between devices  52 us (8%)
  waiting for transfers between devices  34.3 us (5%)
  loops' own time  8.53 us (1%)
    gather x4, local copies, waits for them, and re-layouts, edge_group(): jnp.take(send_proj, senders, axis=0).astype(jnp.float32)  231 us
    dot_general x4, matrix products, edge_group(): jnp.dot(edge_hidden, pe_w2, preferred_element_type=jnp.float32)  55.8 us
    reduce_sum x9, other arithmetic, layer_norm(): spread = jnp.mean(centred * centred, axis=-1, keepdims=True)  48.5 us
    ppermute x16, starting transfers between devices, from_behind(): lax.ppermute(value, axis, [(source, source + steps) for source in range(f...  46 us
    dot_general x4, matrix products, edge_group(): jnp.dot(enc_hidden, enc_w2, preferred_element_type=jnp.float32)  45.2 us
    add x4, other arithmetic, edge_group(): encoded + edge_gain * layer_norm(jnp.dot(edge_hidden, pe_w2, preferred_el...  44.5 us
    ppermute x16, waiting for transfers between devices, from_behind(): lax.ppermute(value, axis, [(source, source + steps) for source in range(f...  34.3 us
    dot_general x4, matrix products, edge_group(): jnp.einsum('get,gtd->ged', picks.astype(jnp.bfloat16), tile_proj, preferr...  22.3 us
  transfers between devices with their start and end apart: 18, of which 8 were waited for; matrix products, arithmetic and copies ran while one was open for 3% of the time, Pallas kernels for 0%

commit v1 on v0

v1 whole, which is shorter than its diff:
```python
import jax
import jax.numpy as jnp
from jax import lax
from jax.experimental import pallas as pl
from jax.experimental.pallas import tpu as pltpu
from jax.sharding import PartitionSpec as P

BCOLS = 4
MCAP = 128
TILE = 128
EDGES = 2048
HALF = 1024
QUART = 512
PARTS = 4096
GHOST = 5120
STEP_ROW = (-1, -1, -1, 0, 0, 1, 1, 1)
STEP_COL = (-1, 0, 1, -1, 1, -1, 0, 1)
EPS = 1e-05
F32 = jnp.float32
BF16 = jnp.bfloat16


def from_behind(value, axis, steps):
    count = lax.axis_size(axis)
    first, last = (max(0, -steps), min(count, count - steps))
    return lax.ppermute(value, axis, [(source, source + steps) for source in range(first, last)])


def dot(a, b):
    return jnp.dot(a, b, preferred_element_type=F32)


def iota(shape, dim):
    return lax.broadcasted_iota(jnp.int32, shape, dim)


def edge_kernel(
    brick_ref,
    geom_ref,
    recv_ref,
    own_ref,
    ext_ref,
    dest_ref,
    send_hbm,
    enc_w1_ref,
    enc_b1_ref,
    enc_w2_ref,
    pe_w1_ref,
    pe_w2_ref,
    edge_gain_ref,
    pn_w1_ref,
    pn_w2_ref,
    node_gain_ref,
    staying_ref,
    outgoing_ref,
    table,
    w_first,
    w_enc,
    w_msg,
    w_mean,
    w_before,
    w_node,
    counts,
    leaving,
    send_a,
    send_b,
    sems,
):
    step = pl.program_id(0)
    steps = pl.num_programs(0)

    def fetch(slot, which, at):
        return pltpu.make_async_copy(
            send_hbm.at[:, pl.ds(at * EDGES + which * HALF, HALF)], slot, sems.at[which]
        )

    @pl.when(step == 0)
    def _():
        fetch(send_a, 0, 0).start()
        fetch(send_b, 1, 0).start()
        w_first[...] = jnp.zeros_like(w_first)
        w_enc[...] = jnp.zeros_like(w_enc)
        w_msg[...] = jnp.zeros_like(w_msg)
        w_mean[...] = jnp.zeros_like(w_mean)
        counts[...] = jnp.zeros_like(counts)
        leaving[...] = jnp.zeros_like(leaving)
        row8 = iota((8, 128), 0)
        weights = jnp.zeros((8, 128), F32)
        for c in range(4):
            weights = jnp.where(row8 == c, enc_w1_ref[c : c + 1, :], weights)
        weights = jnp.where(row8 == 4, enc_b1_ref[0:1, :], weights)
        high = weights.astype(BF16).astype(F32)
        low = weights - high
        pick = jnp.where(row8 == 5, 1.0, 0.0).astype(F32)
        zero = jnp.zeros((8, 128), F32)
        w_first[:, 0:128] = jnp.concatenate([high, high, low, zero], axis=0).astype(BF16)
        w_first[:, 128:256] = jnp.concatenate([pick, zero, zero, zero], axis=0).astype(BF16)

        def centred(ref):
            full = ref[...].astype(F32)
            return (full - jnp.mean(full, axis=1, keepdims=True)).astype(BF16)

        enc = centred(enc_w2_ref)
        msg = centred(pe_w2_ref)
        mean = jnp.full((128, 128), 1.0 / 128, BF16)
        for k in (0, 128):
            w_enc[k : k + 128, k : k + 128] = enc
            w_msg[k : k + 128, k : k + 128] = msg
            w_mean[k : k + 128, k : k + 128] = mean
        w_node[...] = centred(pn_w2_ref)
        w_before[0:128, :] = pe_w1_ref[0]

        @pl.loop(0, (PARTS + GHOST) // 512)
        def _(i):
            at = pl.multiple_of(i * 512, 512)
            block = dot(ext_ref[pl.ds(at, 512), :], pe_w1_ref[2])
            table[pl.ds(at, 512), :] = block.astype(BF16).astype(F32)

    own = own_ref[...]
    w_before[128:256, :] = dot(own, pe_w1_ref[1]).astype(BF16)

    row8 = iota((8, 128), 0)
    lane = iota((HALF, 128), 1).astype(F32)
    rows = iota((TILE, HALF), 0)

    def gathered(slot, first, count):
        blocks = []
        for at in range(first, first + count, 8):
            block = jnp.broadcast_to(table[pl.ds(slot[0, at], 1), :], (8, 128))
            for s in range(1, 8):
                line = jnp.broadcast_to(table[pl.ds(slot[0, at + s], 1), :], (8, 128))
                block = jnp.where(row8 == s, line, block)
            blocks.append(block)
        return jnp.concatenate(blocks, axis=0)

    def normed(values):
        half = values.astype(BF16)
        spread = dot(half * half, w_mean[...])
        return (values * lax.rsqrt(spread + EPS)).astype(BF16)

    def half_tile(which, slot):
        at = which * HALF
        geom = geom_ref[0, :, at : at + HALF]
        local = recv_ref[:, at : at + HALF] - step * TILE
        length = jnp.sqrt(geom[0:1] * geom[0:1] + geom[1:2] * geom[1:2] + geom[2:3] * geom[2:3])
        r8 = iota((8, HALF), 0)
        feats = jnp.where(r8 == 4, 1.0, jnp.zeros((8, HALF), F32))
        for c in range(3):
            feats = jnp.where(r8 == c, geom[c : c + 1], feats)
        feats = jnp.where(r8 == 3, length, feats)
        feats = jnp.where(r8 == 5, local.astype(F32), feats)
        high = feats.astype(BF16).astype(F32)
        low = feats - high
        feats = jnp.concatenate([high, low, high, jnp.zeros_like(high)], axis=0).astype(BF16)
        both = lax.dot_general(
            feats, w_first[...], (((0,), (0,)), ((), ())), preferred_element_type=F32
        )
        hidden = jnp.maximum(both[:, 0:128], 0.0).astype(BF16)
        picks = jnp.where(both[:, 128:256] == lane, 1.0, 0.0).astype(BF16)
        paired = jnp.concatenate([hidden[0:QUART], hidden[QUART:HALF]], axis=1)
        encoded = normed(dot(paired, w_enc[...]))
        left = dot(
            jnp.concatenate([encoded[:, 0:128], picks[0:QUART]], axis=1), w_before[...]
        ) + gathered(slot, 0, QUART)
        right = dot(
            jnp.concatenate([encoded[:, 128:256], picks[QUART:HALF]], axis=1), w_before[...]
        ) + gathered(slot, QUART, QUART)
        paired = jnp.maximum(jnp.concatenate([left, right], axis=1), 0.0).astype(BF16)
        message = normed(dot(paired, w_msg[...]))
        picks_t = jnp.where(rows == local, 1.0, 0.0).astype(BF16)
        joined = jnp.concatenate(
            [
                jnp.concatenate([encoded[:, 0:128], encoded[:, 128:256]], axis=0),
                jnp.concatenate([message[:, 0:128], message[:, 128:256]], axis=0),
            ],
            axis=1,
        )
        return dot(picks_t, joined)

    fetch(send_a, 0, step).wait()
    total = half_tile(0, send_a)

    @pl.when(step + 1 < steps)
    def _():
        fetch(send_a, 0, step + 1).start()

    fetch(send_b, 1, step).wait()
    total += half_tile(1, send_b)

    @pl.when(step + 1 < steps)
    def _():
        fetch(send_b, 1, step + 1).start()

    aggregate = (total[:, 0:128] + edge_gain_ref[0:1, :] * total[:, 128:256]).astype(BF16)
    node = jnp.maximum(dot(own, pn_w1_ref[0]) + dot(aggregate, pn_w1_ref[1]), 0.0).astype(BF16)
    node = dot(node, w_node[...])
    spread = jnp.mean(node * node, axis=1, keepdims=True)
    node = node * lax.rsqrt(spread + EPS)
    updated = (own.astype(F32) + node_gain_ref[0:1, :] * node).astype(BF16)

    brick = brick_ref[0]
    dest = dest_ref[...]
    eye = iota((TILE, TILE), 0) == iota((TILE, TILE), 1)
    stays = jnp.where(eye & (dest == brick), 1.0, 0.0).astype(BF16)
    staying_ref[...] = dot(stays, updated).astype(BF16)
    k8 = iota((8, TILE), 0)
    k9 = jnp.where(k8 >= 4, k8 + 1, k8)
    move_row = dest // BCOLS - brick // BCOLS
    move_col = dest % BCOLS - brick % BCOLS
    code = (move_row + 1) * 3 + move_col + 1
    heads = jnp.where(code == k9, 1.0, 0.0)
    upper = jnp.where(iota((TILE, TILE), 0) <= iota((TILE, TILE), 1), 1.0, 0.0).astype(BF16)
    running = dot(heads.astype(BF16), upper) + counts[...]
    counts[...] += jnp.sum(heads, axis=1, keepdims=True)
    slots = jnp.sum(
        heads * (running + (k8 * MCAP).astype(F32)), axis=0, keepdims=True
    ).astype(jnp.int32) - 1
    chosen = jnp.where(iota((8 * MCAP, TILE), 0) == slots, 1.0, 0.0).astype(BF16)
    leaving[...] += dot(chosen, updated)

    @pl.when(step == steps - 1)
    def _():
        outgoing_ref[...] = leaving[...].astype(BF16)


def edge_call(brick, geom, recv, own, ext, dest, send, params):
    steps = PARTS // TILE
    whole = lambda shape: pl.BlockSpec(shape, lambda i, _: (0,) * len(shape))
    return pl.pallas_call(
        edge_kernel,
        grid_spec=pltpu.PrefetchScalarGridSpec(
            num_scalar_prefetch=1,
            grid=(steps,),
            in_specs=[
                pl.BlockSpec((1, 3, EDGES), lambda i, _: (0, 0, i)),
                pl.BlockSpec((1, EDGES), lambda i, _: (0, i)),
                pl.BlockSpec((TILE, 128), lambda i, _: (i, 0)),
                whole((PARTS + GHOST, 128)),
                pl.BlockSpec((1, TILE), lambda i, _: (0, i)),
                pl.BlockSpec(memory_space=pl.ANY),
                whole((4, 128)),
                whole((1, 128)),
                whole((128, 128)),
                whole((3, 128, 128)),
                whole((128, 128)),
                whole((1, 128)),
                whole((2, 128, 128)),
                whole((128, 128)),
                whole((1, 128)),
            ],
            out_specs=[
                pl.BlockSpec((TILE, 128), lambda i, _: (i, 0)),
                whole((8 * MCAP, 128)),
            ],
            scratch_shapes=[
                pltpu.VMEM((PARTS + GHOST, 128), F32),
                pltpu.VMEM((32, 256), BF16),
                pltpu.VMEM((256, 256), BF16),
                pltpu.VMEM((256, 256), BF16),
                pltpu.VMEM((256, 256), BF16),
                pltpu.VMEM((256, 128), BF16),
                pltpu.VMEM((128, 128), BF16),
                pltpu.VMEM((8, 128), F32),
                pltpu.VMEM((8 * MCAP, 128), F32),
                pltpu.SMEM((1, HALF), jnp.int32),
                pltpu.SMEM((1, HALF), jnp.int32),
                pltpu.SemaphoreType.DMA((2,)),
            ],
        ),
        out_shape=[
            jax.ShapeDtypeStruct((PARTS, 128), BF16),
            jax.ShapeDtypeStruct((8 * MCAP, 128), BF16),
        ],
        compiler_params=pltpu.CompilerParams(vmem_limit_bytes=40 << 20),
        cost_estimate=pl.CostEstimate(
            flops=9_000_000_000, bytes_accessed=6_000_000, transcendentals=1_000_000
        ),
    )(brick, geom, recv, own, ext, dest, send, *params)


def shifted(blocks):
    return jnp.stack(
        [
            from_behind(blocks[k], "floor", STEP_ROW[k] * BCOLS + STEP_COL[k])
            for k in range(8)
        ]
    )


def per_device(
    latent,
    edge_geom,
    edge_recv,
    edge_send,
    ghost_rows,
    dest,
    enc_w1,
    enc_b1,
    enc_w2,
    pe_w1,
    pe_w2,
    edge_gain,
    pn_w1,
    pn_w2,
    node_gain,
):
    own = latent[0]
    brick = lax.axis_index("floor").astype(jnp.int32)
    packets = jnp.take(own, ghost_rows[0].reshape(-1), axis=0).reshape(10, 512, 128)
    floor_blocks = shifted(packets[:8]).reshape(8 * 512, 128)
    above = from_behind(packets[8], "slab", -1)
    below = from_behind(packets[9], "slab", 1)
    ext = jnp.concatenate([own, floor_blocks, above, below], axis=0)
    params = (
        enc_w1,
        enc_b1.reshape(1, 128),
        enc_w2,
        pe_w1,
        pe_w2,
        edge_gain.reshape(1, 128),
        pn_w1,
        pn_w2,
        node_gain.reshape(1, 128),
    )
    staying, outgoing = edge_call(
        brick.reshape(1), edge_geom, edge_recv, own, ext, dest, edge_send, params
    )
    arrived = shifted(outgoing.reshape(8, MCAP, 128))
    return (staying[None], arrived[None])


def solution(mesh):
    in_specs = (
        P("slab", "floor", None),
        P("slab", None, "floor"),
        P("slab", "floor"),
        P("slab", "floor"),
        P("slab", "floor", None),
        P("slab", "floor"),
    ) + (P(),) * 9
    out_specs = (P("slab", "floor", None), P("slab", "floor", None, None))
    return jax.shard_map(
        per_device, mesh=mesh, in_specs=in_specs, out_specs=out_specs, check_vma=False
    )
```

time: 677 us -> 279 us (0.41)
  the two profiles are of different devices: /device:TPU:1 before, /device:TPU:30 now
where the time goes in v1:
time: 279 us
  Pallas kernels  142 us (51%)
  starting transfers between devices  52.1 us (19%)
  waiting for transfers between devices  43.7 us (16%)
  other arithmetic  20.6 us (7%)
  local copies, waits for them, and re-layouts  18.6 us (7%)
    pallas_call x1, Pallas kernels, edge_call(): pl.pallas_call(edge_kernel, grid_spec=pltpu.PrefetchScalarGridSpec(num_sc...  142 us
    ppermute x18, starting transfers between devices, from_behind(): lax.ppermute(value, axis, [(source, source + steps) for source in range(f...  52.1 us
    ppermute x18, waiting for transfers between devices, from_behind(): lax.ppermute(value, axis, [(source, source + steps) for source in range(f...  43.7 us
    concatenate x1, other arithmetic, per_device(): ext = jnp.concatenate([own, floor_blocks, above, below], axis=0)  16.4 us
    gather x1, local copies, waits for them, and re-layouts, per_device(): jnp.take(own, ghost_rows[0].reshape(-1), axis=0).reshape(10, 512, 128)  15.1 us
  transfers between devices with their start and end apart: 18, of which 8 were waited for; matrix products, arithmetic and copies ran while one was open for 1% of the time, Pallas kernels for 0%

profile of v1, /device:TPU:30, one launch (start us, length us, event | category | flops | bytes accessed | tf_op | source)
XLA Modules:
  0.0 278.6 jit_solution(17615609808787712133)
XLA Ops:
  2.1 15.1 %gather_fusion = bf16[5120,128]{1,0:T(8,128)(2,1)S(1)} fusion(bf16[4096,128]{1,0:T(8,128)(2,1)} %bitcast.43, s32[5120]{0:T(1024)S(1)} %broadcast_clamp_fusion), kind=kCustom, calls=%fused_computation | custom fusion | bytes 2641920 | tf_op jit(solution)/shard_map/jit(_take)/gather | solution.py:309
  17.3 2.7 broadcast_select_fusion
  21.5 8.2 %collective-permute-start.7 = (bf16[512,128]{1,0:T(8,128)(2,1)S(1)}, bf16[512,128]{1,0:T(8,128)(2,1)S(1)}, u32[]{:S(2)}, u32[]{:S(2)}) collective-permute-start(bf16[512,128]{1,0:T(8,128)(2,1)S(1)} %get-tuple-element.6), channel_id=1, source_target_pairs={{0,40},{8,48},{16,56},{24,64},{32,72},{40,80},{48,88},{56,96},{64,... | collective-permute-start | bytes 393224 | tf_op jit(solution)/shard_map/ppermute | solution.py:26
  29.7 1.9 collective-permute-start.9
  31.6 3.6 %collective-permute-start.8 = (bf16[512,128]{1,0:T(8,128)(2,1)S(1)}, bf16[512,128]{1,0:T(8,128)(2,1)S(1)}, u32[]{:S(2)}, u32[]{:S(2)}) collective-permute-start(bf16[512,128]{1,0:T(8,128)(2,1)S(1)} %get-tuple-element.8), channel_id=1, source_target_pairs={{1,0},{2,1},{3,2},{4,3},{5,4},{6,5},{7,6},{9,8},{10,9},{11,10},{12... | collective-permute-start | bytes 393224 | tf_op jit(solution)/shard_map/ppermute | solution.py:26
  35.2 5.1 %collective-permute-start.6 = (bf16[512,128]{1,0:T(8,128)(2,1)S(1)}, bf16[512,128]{1,0:T(8,128)(2,1)}, u32[]{:S(2)}, u32[]{:S(2)}) collective-permute-start(bf16[512,128]{1,0:T(8,128)(2,1)S(1)} %get-tuple-element.9), channel_id=1, source_target_pairs={{0,32},{8,40},{16,48},{24,56},{32,64},{40,72},{48,80},{56,88},{64,... | collective-permute-start | bytes 393224 | tf_op jit(solution)/shard_map/ppermute | solution.py:26
  43.1 4.6 %collective-permute-done.1 = bf16[512,128]{1,0:T(8,128)(2,1)S(1)} collective-permute-done((bf16[512,128]{1,0:T(8,128)(2,1)S(1)}, bf16[512,128]{1,0:T(8,128)(2,1)S(1)}, u32[]{:S(2)}, u32[]{:S(2)}) %collective-permute-start.1) | collective-permute-done | bytes 131104 | tf_op jit(solution)/shard_map/ppermute | solution.py:26
  47.8 1.9 collective-permute-start.2
  49.7 5.8 %collective-permute-done.2 = bf16[512,128]{1,0:T(8,128)(2,1)S(1)} collective-permute-done((bf16[512,128]{1,0:T(8,128)(2,1)S(1)}, bf16[512,128]{1,0:T(8,128)(2,1)S(1)}, u32[]{:S(2)}, u32[]{:S(2)}) %collective-permute-start.2) | collective-permute-done | bytes 131104 | tf_op jit(solution)/shard_map/ppermute | solution.py:26
  55.5 1.9 collective-permute-start.3
  57.4 7.0 %collective-permute-done.3 = bf16[512,128]{1,0:T(8,128)(2,1)S(1)} collective-permute-done((bf16[512,128]{1,0:T(8,128)(2,1)S(1)}, bf16[512,128]{1,0:T(8,128)(2,1)S(1)}, u32[]{:S(2)}, u32[]{:S(2)}) %collective-permute-start.3) | collective-permute-done | bytes 131104 | tf_op jit(solution)/shard_map/ppermute | solution.py:26
  64.5 1.9 collective-permute-start.4
  66.4 4.9 %collective-permute-done.4 = bf16[512,128]{1,0:T(8,128)(2,1)S(1)} collective-permute-done((bf16[512,128]{1,0:T(8,128)(2,1)S(1)}, bf16[512,128]{1,0:T(8,128)(2,1)S(1)}, u32[]{:S(2)}, u32[]{:S(2)}) %collective-permute-start.4) | collective-permute-done | bytes 131104 | tf_op jit(solution)/shard_map/ppermute | solution.py:26
  71.3 1.9 collective-permute-start.5
  73.3 6.1 %collective-permute-done.5 = bf16[512,128]{1,0:T(8,128)(2,1)S(1)} collective-permute-done((bf16[512,128]{1,0:T(8,128)(2,1)S(1)}, bf16[512,128]{1,0:T(8,128)(2,1)S(1)}, u32[]{:S(2)}, u32[]{:S(2)}) %collective-permute-start.5) | collective-permute-done | bytes 131104 | tf_op jit(solution)/shard_map/ppermute | solution.py:26
  80.5 16.4 %pad_maximum_fusion.ext_ref = bf16[9216,128]{1,0:T(8,128)(2,1)S(1)} fusion(bf16[512,128]{1,0:T(8,128)(2,1)S(1)} %collective-permute-done.9, bf16[512,128]{1,0:T(8,128)(2,1)S(1)} %collective-permute-done.8, bf16[4096,128]{1,0:T(8,128)(2,1)S(1)} %bitcast.49, bf16[4096,128]{1,0:T(8,128)(2,1)S(1)} %bitcast.44), kind=kLoop, calls=%fused_computation.1 | loop fusion | flops 9437184 | bytes 4718592 | tf_op jit(solution)/shard_map/concatenate | solution.py:313
  97.1 142.4 %shard_map.158 = (bf16[4096,128]{1,0:T(8,128)(2,1)}, bf16[1024,128]{1,0:T(8,128)(2,1)S(1)}) custom-call(s32[1]{0:T(128)} %bitcast.brick_ref, f32[1,3,65536]{2,1,0:T(4,128)S(1)} %copy.17.geom_ref, s32[1,65536]{1,0:T(1,128)S(1)} %copy-done.1, bf16[4096,128]{1,0:T(8,128)(2,1)S(1)} %bitcast.45, bf16[9216,128]{1,0:T(8,128)(2,1)S(1)} %pad_maximum_fusion.ext_ref, ...), custom_call_target="tpu_custom_call" | custom-call | flops 8999999488 | bytes 6000000 | tf_op jit(solution)/shard_map/pallas_call | solution.py:229
  240.8 8.2 %collective-permute-start.17 = (bf16[128,128]{1,0:T(8,128)(2,1)S(1)}, bf16[128,128]{1,0:T(8,128)(2,1)S(1)}, u32[]{:S(2)}, u32[]{:S(2)}) collective-permute-start(bf16[128,128]{1,0:T(8,128)(2,1)S(1)} %get-tuple-element.16), channel_id=1, source_target_pairs={{0,40},{8,48},{16,56},{24,64},{32,72},{40,80},{48,88},{56,96},{64,... | collective-permute-start | bytes 98312 | tf_op jit(solution)/shard_map/ppermute | solution.py:26
  250.8 1.9 collective-permute-start.15
  252.8 4.6 %collective-permute-start.14 = (bf16[128,128]{1,0:T(8,128)(2,1)S(1)}, bf16[128,128]{1,0:T(8,128)(2,1)S(1)}, u32[]{:S(2)}, u32[]{:S(2)}) collective-permute-start(bf16[128,128]{1,0:T(8,128)(2,1)S(1)} %get-tuple-element.19), channel_id=1, source_target_pairs={{0,8},{8,16},{16,24},{24,32},{32,40},{40,48},{48,56},{56,64},{64,7... | collective-permute-start | bytes 98312 | tf_op jit(solution)/shard_map/ppermute | solution.py:26
  258.7 4.5 %collective-permute-done.11 = bf16[128,128]{1,0:T(8,128)(2,1)S(1)} collective-permute-done((bf16[128,128]{1,0:T(8,128)(2,1)S(1)}, bf16[128,128]{1,0:T(8,128)(2,1)S(1)}, u32[]{:S(2)}, u32[]{:S(2)}) %collective-permute-start.11) | collective-permute-done | bytes 32800 | tf_op jit(solution)/shard_map/ppermute | solution.py:26
  265.1 4.8 %collective-permute-done.12 = bf16[128,128]{1,0:T(8,128)(2,1)S(1)} collective-permute-done((bf16[128,128]{1,0:T(8,128)(2,1)S(1)}, bf16[128,128]{1,0:T(8,128)(2,1)S(1)}, u32[]{:S(2)}, u32[]{:S(2)}) %collective-permute-start.12) | collective-permute-done | bytes 32800 | tf_op jit(solution)/shard_map/ppermute | solution.py:26
  269.9 1.9 collective-permute-start.13
  271.8 6.0 %collective-permute-done.13 = bf16[128,128]{1,0:T(8,128)(2,1)S(1)} collective-permute-done((bf16[128,128]{1,0:T(8,128)(2,1)S(1)}, bf16[128,128]{1,0:T(8,128)(2,1)S(1)}, u32[]{:S(2)}, u32[]{:S(2)}) %collective-permute-start.13) | collective-permute-done | bytes 32800 | tf_op jit(solution)/shard_map/ppermute | solution.py:26
  (68 shorter events, 14.0 us)
Async XLA Ops:
  17.2 23.1 %copy-start.13 = (f32[1,3,65536]{2,0,1:T(1,128)S(1)}, f32[1,3,65536]{2,0,1:T(1,128)}, u32[]{:S(2)}) copy-start(f32[1,3,65536]{2,0,1:T(1,128)} %param.16) | copy-start | bytes 2359300
  20.0 60.4 %copy-start = (bf16[1,4096,128]{2,1,0:T(8,128)(2,1)S(1)}, bf16[1,4096,128]{2,1,0:T(8,128)(2,1)}, u32[]{:S(2)}) copy-start(bf16[1,4096,128]{2,1,0:T(8,128)(2,1)} %param.15) | copy-start | bytes 3145732
  20.1 20.8 %collective-permute-start = (bf16[512,128]{1,0:T(8,128)(2,1)S(1)}, bf16[512,128]{1,0:T(8,128)(2,1)}, u32[]{:S(2)}, u32[]{:S(2)}) collective-permute-start(bf16[512,128]{1,0:T(8,128)(2,1)S(1)} %get-tuple-element.15), channel_id=1, source_target_pairs={{40,0},{48,8},{56,16},{64,24},{72,32},{80,40},{88,48},{96,56},{104... | collective-permute-start | bytes 393224 | tf_op jit(solution)/shard_map/ppermute | solution.py:26
  21.5 58.9 %collective-permute-start.7 = (bf16[512,128]{1,0:T(8,128)(2,1)S(1)}, bf16[512,128]{1,0:T(8,128)(2,1)S(1)}, u32[]{:S(2)}, u32[]{:S(2)}) collective-permute-start(bf16[512,128]{1,0:T(8,128)(2,1)S(1)} %get-tuple-element.6), channel_id=1, source_target_pairs={{0,40},{8,48},{16,56},{24,64},{32,72},{40,80},{48,88},{56,96},{64,... | collective-permute-start | bytes 393224 | tf_op jit(solution)/shard_map/ppermute | solution.py:26
  29.7 50.7 %collective-permute-start.9 = (bf16[512,128]{1,0:T(8,128)(2,1)S(1)}, bf16[512,128]{1,0:T(8,128)(2,1)S(1)}, u32[]{:S(2)}, u32[]{:S(2)}) collective-permute-start(bf16[512,128]{1,0:T(8,128)(2,1)S(1)} %get-tuple-element.7), channel_id=1, source_target_pairs={{0,1},{1,2},{2,3},{3,4},{4,5},{5,6},{6,7},{8,9},{9,10},{10,11},{11... | collective-permute-start | bytes 393224 | tf_op jit(solution)/shard_map/ppermute | solution.py:26
  31.6 48.8 %collective-permute-start.8 = (bf16[512,128]{1,0:T(8,128)(2,1)S(1)}, bf16[512,128]{1,0:T(8,128)(2,1)S(1)}, u32[]{:S(2)}, u32[]{:S(2)}) collective-permute-start(bf16[512,128]{1,0:T(8,128)(2,1)S(1)} %get-tuple-element.8), channel_id=1, source_target_pairs={{1,0},{2,1},{3,2},{4,3},{5,4},{6,5},{7,6},{9,8},{10,9},{11,10},{12... | collective-permute-start | bytes 393224 | tf_op jit(solution)/shard_map/ppermute | solution.py:26
  35.2 44.2 %collective-permute-start.6 = (bf16[512,128]{1,0:T(8,128)(2,1)S(1)}, bf16[512,128]{1,0:T(8,128)(2,1)}, u32[]{:S(2)}, u32[]{:S(2)}) collective-permute-start(bf16[512,128]{1,0:T(8,128)(2,1)S(1)} %get-tuple-element.9), channel_id=1, source_target_pairs={{0,32},{8,40},{16,48},{24,56},{32,64},{40,72},{48,80},{56,88},{64,... | collective-permute-start | bytes 393224 | tf_op jit(solution)/shard_map/ppermute | solution.py:26
  40.9 6.9 %collective-permute-start.1 = (bf16[512,128]{1,0:T(8,128)(2,1)S(1)}, bf16[512,128]{1,0:T(8,128)(2,1)S(1)}, u32[]{:S(2)}, u32[]{:S(2)}) collective-permute-start(bf16[512,128]{1,0:T(8,128)(2,1)S(1)} %get-tuple-element.14), channel_id=1, source_target_pairs={{32,0},{40,8},{48,16},{56,24},{64,32},{72,40},{80,48},{88,56},{96,... | collective-permute-start | bytes 393224 | tf_op jit(solution)/shard_map/ppermute | solution.py:26
  47.8 7.7 %collective-permute-start.2 = (bf16[512,128]{1,0:T(8,128)(2,1)S(1)}, bf16[512,128]{1,0:T(8,128)(2,1)S(1)}, u32[]{:S(2)}, u32[]{:S(2)}) collective-permute-start(bf16[512,128]{1,0:T(8,128)(2,1)S(1)} %get-tuple-element.13), channel_id=1, source_target_pairs={{24,0},{32,8},{40,16},{48,24},{56,32},{64,40},{72,48},{80,56},{88,... | collective-permute-start | bytes 393224 | tf_op jit(solution)/shard_map/ppermute | solution.py:26
  55.5 9.0 %collective-permute-start.3 = (bf16[512,128]{1,0:T(8,128)(2,1)S(1)}, bf16[512,128]{1,0:T(8,128)(2,1)S(1)}, u32[]{:S(2)}, u32[]{:S(2)}) collective-permute-start(bf16[512,128]{1,0:T(8,128)(2,1)S(1)} %get-tuple-element.12), channel_id=1, source_target_pairs={{8,0},{16,8},{24,16},{32,24},{40,32},{48,40},{56,48},{64,56},{72,6... | collective-permute-start | bytes 393224 | tf_op jit(solution)/shard_map/ppermute | solution.py:26
  64.5 6.8 %collective-permute-start.4 = (bf16[512,128]{1,0:T(8,128)(2,1)S(1)}, bf16[512,128]{1,0:T(8,128)(2,1)S(1)}, u32[]{:S(2)}, u32[]{:S(2)}) collective-permute-start(bf16[512,128]{1,0:T(8,128)(2,1)S(1)} %get-tuple-element.11), channel_id=1, source_target_pairs={{0,8},{8,16},{16,24},{24,32},{32,40},{40,48},{48,56},{56,64},{64,7... | collective-permute-start | bytes 393224 | tf_op jit(solution)/shard_map/ppermute | solution.py:26
  71.3 8.1 %collective-permute-start.5 = (bf16[512,128]{1,0:T(8,128)(2,1)S(1)}, bf16[512,128]{1,0:T(8,128)(2,1)S(1)}, u32[]{:S(2)}, u32[]{:S(2)}) collective-permute-start(bf16[512,128]{1,0:T(8,128)(2,1)S(1)} %get-tuple-element.10), channel_id=1, source_target_pairs={{0,24},{8,32},{16,40},{24,48},{32,56},{40,64},{48,72},{56,80},{64,... | collective-permute-start | bytes 393224 | tf_op jit(solution)/shard_map/ppermute | solution.py:26
  80.4 16.6 %copy-start.1 = (s32[1,65536]{1,0:T(1,128)S(1)}, s32[1,65536]{1,0:T(1,128)}, u32[]{:S(2)}) copy-start(s32[1,65536]{1,0:T(1,128)} %recv_ref.1) | copy-start | bytes 786436
  80.4 16.6 %copy-start.2 = (s32[1,65536]{1,0:T(1,128)S(1)}, s32[1,65536]{1,0:T(1,128)}, u32[]{:S(2)}) copy-start(s32[1,65536]{1,0:T(1,128)} %send_hbm.1) | copy-start | bytes 786436
  80.4 16.6 %copy-start.3 = (bf16[3,128,128]{2,1,0:T(8,128)(2,1)S(1)}, bf16[3,128,128]{2,1,0:T(8,128)(2,1)}, u32[]{:S(2)}) copy-start(bf16[3,128,128]{2,1,0:T(8,128)(2,1)} %pe_w1_ref.1) | copy-start | bytes 294916
  80.4 16.6 %copy-start.4 = (bf16[2,128,128]{2,1,0:T(8,128)(2,1)S(1)}, bf16[2,128,128]{2,1,0:T(8,128)(2,1)}, u32[]{:S(2)}) copy-start(bf16[2,128,128]{2,1,0:T(8,128)(2,1)} %pn_w1_ref.1) | copy-start | bytes 196612
  239.5 17.8 %collective-permute-start.10 = (bf16[128,128]{1,0:T(8,128)(2,1)S(1)}, bf16[128,128]{1,0:T(8,128)(2,1)S(1)}, u32[]{:S(2)}, u32[]{:S(2)}) collective-permute-start(bf16[128,128]{1,0:T(8,128)(2,1)S(1)} %get-tuple-element.23), channel_id=1, source_target_pairs={{40,0},{48,8},{56,16},{64,24},{72,32},{80,40},{88,48},{96,56},{104... | collective-permute-start | bytes 98312 | tf_op jit(solution)/shard_map/ppermute | solution.py:26
  240.8 37.0 %collective-permute-start.17 = (bf16[128,128]{1,0:T(8,128)(2,1)S(1)}, bf16[128,128]{1,0:T(8,128)(2,1)S(1)}, u32[]{:S(2)}, u32[]{:S(2)}) collective-permute-start(bf16[128,128]{1,0:T(8,128)(2,1)S(1)} %get-tuple-element.16), channel_id=1, source_target_pairs={{0,40},{8,48},{16,56},{24,64},{32,72},{40,80},{48,88},{56,96},{64,... | collective-permute-start | bytes 98312 | tf_op jit(solution)/shard_map/ppermute | solution.py:26
  249.0 28.8 %collective-permute-start.16 = (bf16[128,128]{1,0:T(8,128)(2,1)S(1)}, bf16[128,128]{1,0:T(8,128)(2,1)S(1)}, u32[]{:S(2)}, u32[]{:S(2)}) collective-permute-start(bf16[128,128]{1,0:T(8,128)(2,1)S(1)} %get-tuple-element.17), channel_id=1, source_target_pairs={{0,32},{8,40},{16,48},{24,56},{32,64},{40,72},{48,80},{56,88},{64,... | collective-permute-start | bytes 98312 | tf_op jit(solution)/shard_map/ppermute | solution.py:26
  250.8 27.0 %collective-permute-start.15 = (bf16[128,128]{1,0:T(8,128)(2,1)S(1)}, bf16[128,128]{1,0:T(8,128)(2,1)S(1)}, u32[]{:S(2)}, u32[]{:S(2)}) collective-permute-start(bf16[128,128]{1,0:T(8,128)(2,1)S(1)} %get-tuple-element.18), channel_id=1, source_target_pairs={{0,24},{8,32},{16,40},{24,48},{32,56},{40,64},{48,72},{56,80},{64,... | collective-permute-start | bytes 98312 | tf_op jit(solution)/shard_map/ppermute | solution.py:26
  252.8 25.0 %collective-permute-start.14 = (bf16[128,128]{1,0:T(8,128)(2,1)S(1)}, bf16[128,128]{1,0:T(8,128)(2,1)S(1)}, u32[]{:S(2)}, u32[]{:S(2)}) collective-permute-start(bf16[128,128]{1,0:T(8,128)(2,1)S(1)} %get-tuple-element.19), channel_id=1, source_target_pairs={{0,8},{8,16},{16,24},{24,32},{32,40},{40,48},{48,56},{56,64},{64,7... | collective-permute-start | bytes 98312 | tf_op jit(solution)/shard_map/ppermute | solution.py:26
  257.4 5.8 %collective-permute-start.11 = (bf16[128,128]{1,0:T(8,128)(2,1)S(1)}, bf16[128,128]{1,0:T(8,128)(2,1)S(1)}, u32[]{:S(2)}, u32[]{:S(2)}) collective-permute-start(bf16[128,128]{1,0:T(8,128)(2,1)S(1)} %get-tuple-element.22), channel_id=1, source_target_pairs={{32,0},{40,8},{48,16},{56,24},{64,32},{72,40},{80,48},{88,56},{96,... | collective-permute-start | bytes 98312 | tf_op jit(solution)/shard_map/ppermute | solution.py:26
  263.2 6.7 %collective-permute-start.12 = (bf16[128,128]{1,0:T(8,128)(2,1)S(1)}, bf16[128,128]{1,0:T(8,128)(2,1)S(1)}, u32[]{:S(2)}, u32[]{:S(2)}) collective-permute-start(bf16[128,128]{1,0:T(8,128)(2,1)S(1)} %get-tuple-element.21), channel_id=1, source_target_pairs={{24,0},{32,8},{40,16},{48,24},{56,32},{64,40},{72,48},{80,56},{88,... | collective-permute-start | bytes 98312 | tf_op jit(solution)/shard_map/ppermute | solution.py:26
  269.9 7.9 %collective-permute-start.13 = (bf16[128,128]{1,0:T(8,128)(2,1)S(1)}, bf16[128,128]{1,0:T(8,128)(2,1)S(1)}, u32[]{:S(2)}, u32[]{:S(2)}) collective-permute-start(bf16[128,128]{1,0:T(8,128)(2,1)S(1)} %get-tuple-element.20), channel_id=1, source_target_pairs={{8,0},{16,8},{24,16},{32,24},{40,32},{48,40},{56,48},{64,56},{72,6... | collective-permute-start | bytes 98312 | tf_op jit(solution)/shard_map/ppermute | solution.py:26
  (9 other events, 133.1 us)

commit v2 on v1

--- a/solution.py
+++ b/solution.py
@@ -20,12 +20,6 @@
 BF16 = jnp.bfloat16
 
 
-def from_behind(value, axis, steps):
-    count = lax.axis_size(axis)
-    first, last = (max(0, -steps), min(count, count - steps))
-    return lax.ppermute(value, axis, [(source, source + steps) for source in range(first, last)])
-
-
 def dot(a, b):
     return jnp.dot(a, b, preferred_element_type=F32)
 
@@ -39,7 +33,8 @@
     geom_ref,
     recv_ref,
     own_ref,
-    ext_ref,
+    all_ref,
+    ghost_ref,
     dest_ref,
     send_hbm,
     enc_w1_ref,
@@ -107,14 +102,24 @@
             w_enc[k : k + 128, k : k + 128] = enc
             w_msg[k : k + 128, k : k + 128] = msg
             w_mean[k : k + 128, k : k + 128] = mean
-        w_node[...] = centred(pn_w2_ref)
+        full = pn_w2_ref[...].astype(F32)
+        full = full - jnp.mean(full, axis=1, keepdims=True)
+        high = full.astype(BF16)
+        w_node[0:128, :] = high
+        w_node[128:256, :] = (full - high.astype(F32)).astype(BF16)
         w_before[0:128, :] = pe_w1_ref[0]
 
-        @pl.loop(0, (PARTS + GHOST) // 512)
+        @pl.loop(0, PARTS // 512)
         def _(i):
             at = pl.multiple_of(i * 512, 512)
-            block = dot(ext_ref[pl.ds(at, 512), :], pe_w1_ref[2])
+            block = dot(all_ref[pl.ds(at, 512), :], pe_w1_ref[2])
             table[pl.ds(at, 512), :] = block.astype(BF16).astype(F32)
+
+        @pl.loop(0, GHOST // 512)
+        def _(i):
+            at = pl.multiple_of(i * 512, 512)
+            block = dot(ghost_ref[pl.ds(at, 512), :], pe_w1_ref[2])
+            table[pl.ds(PARTS + at, 512), :] = block.astype(BF16).astype(F32)
 
     own = own_ref[...]
     w_before[128:256, :] = dot(own, pe_w1_ref[1]).astype(BF16)
@@ -193,7 +198,7 @@
 
     aggregate = (total[:, 0:128] + edge_gain_ref[0:1, :] * total[:, 128:256]).astype(BF16)
     node = jnp.maximum(dot(own, pn_w1_ref[0]) + dot(aggregate, pn_w1_ref[1]), 0.0).astype(BF16)
-    node = dot(node, w_node[...])
+    node = dot(jnp.concatenate([node, node], axis=1), w_node[...])
     spread = jnp.mean(node * node, axis=1, keepdims=True)
     node = node * lax.rsqrt(spread + EPS)
     updated = (own.astype(F32) + node_gain_ref[0:1, :] * node).astype(BF16)
@@ -223,7 +228,7 @@
         outgoing_ref[...] = leaving[...].astype(BF16)
 
 
-def edge_call(brick, geom, recv, own, ext, dest, send, params):
+def edge_call(brick, geom, recv, own, ghosts, dest, send, params):
     steps = PARTS // TILE
     whole = lambda shape: pl.BlockSpec(shape, lambda i, _: (0,) * len(shape))
     return pl.pallas_call(
@@ -235,7 +240,8 @@
                 pl.BlockSpec((1, 3, EDGES), lambda i, _: (0, 0, i)),
                 pl.BlockSpec((1, EDGES), lambda i, _: (0, i)),
                 pl.BlockSpec((TILE, 128), lambda i, _: (i, 0)),
-                whole((PARTS + GHOST, 128)),
+                whole((PARTS, 128)),
+                whole((GHOST, 128)),
                 pl.BlockSpec((1, TILE), lambda i, _: (0, i)),
                 pl.BlockSpec(memory_space=pl.ANY),
                 whole((4, 128)),
@@ -259,7 +265,7 @@
                 pltpu.VMEM((256, 256), BF16),
                 pltpu.VMEM((256, 256), BF16),
                 pltpu.VMEM((256, 128), BF16),
-                pltpu.VMEM((128, 128), BF16),
+                pltpu.VMEM((256, 128), BF16),
                 pltpu.VMEM((8, 128), F32),
                 pltpu.VMEM((8 * MCAP, 128), F32),
                 pltpu.SMEM((1, HALF), jnp.int32),
@@ -275,16 +281,168 @@
         cost_estimate=pl.CostEstimate(
             flops=9_000_000_000, bytes_accessed=6_000_000, transcendentals=1_000_000
         ),
-    )(brick, geom, recv, own, ext, dest, send, *params)
-
-
-def shifted(blocks):
-    return jnp.stack(
-        [
-            from_behind(blocks[k], "floor", STEP_ROW[k] * BCOLS + STEP_COL[k])
-            for k in range(8)
-        ]
-    )
+    )(brick, geom, recv, own, own, ghosts, dest, send, *params)
+
+
+MESH = pl.DeviceIdType.MESH
+
+
+def partners(count):
+    floor, slab = lax.axis_index("floor"), lax.axis_index("slab")
+    row, col = floor // BCOLS, floor % BCOLS
+    rows = lax.axis_size("floor") // BCOLS
+    slabs = lax.axis_size("slab")
+
+    def inside(r, c):
+        return (r >= 0) & (r < rows) & (c >= 0) & (c < BCOLS)
+
+    found = []
+    for dr, dc in zip(STEP_ROW, STEP_COL):
+        found.append(
+            (
+                inside(row + dr, col + dc),
+                (floor + dr * BCOLS + dc, slab),
+                inside(row - dr, col - dc),
+            )
+        )
+    found.append((slab >= 1, (floor, slab - 1), slab + 1 < slabs))
+    found.append((slab + 1 < slabs, (floor, slab + 1), slab >= 1))
+    return found[:count]
+
+
+def greet(links):
+    barrier = pltpu.get_barrier_semaphore()
+    for there, device, _ in links:
+
+        @pl.when(there)
+        def _():
+            pl.semaphore_signal(barrier, inc=1, device_id=device, device_id_type=MESH)
+
+    peers = 0
+    for there, _, _ in links:
+        peers = peers + there.astype(jnp.int32)
+    pl.semaphore_wait(barrier, peers)
+
+
+def ghost_kernel(rows_ref, own_ref, ghost_ref, table, packets, send_sems, recv_sems):
+    links = partners(10)
+    row8 = iota((8, 128), 0)
+    ghost_ref[...] = jnp.zeros_like(ghost_ref)
+
+    @pl.loop(0, PARTS // 256)
+    def _(i):
+        at = pl.multiple_of(i * 256, 256)
+        table[pl.ds(at, 256), :] = own_ref[pl.ds(at, 256), :].astype(F32)
+
+    def copy(k, device):
+        block = pl.ds(k * 512, 512)
+        return pltpu.make_async_remote_copy(
+            src_ref=packets.at[block],
+            dst_ref=ghost_ref.at[block],
+            send_sem=send_sems.at[k],
+            recv_sem=recv_sems.at[k],
+            device_id=device,
+            device_id_type=MESH,
+        )
+
+    greet(links)
+    for k in (0, 2, 5, 7, 1, 6, 3, 4, 8, 9):
+        there, device, _ = links[k]
+
+        @pl.loop(0, 8)
+        def _(c):
+            at = pl.multiple_of(c * 64, 64)
+            blocks = []
+            for first in range(0, 64, 8):
+                block = None
+                for s in range(8):
+                    line = jnp.broadcast_to(
+                        table[pl.ds(rows_ref[0, k, at + first + s], 1), :], (8, 128)
+                    )
+                    block = line if s == 0 else jnp.where(row8 == s, line, block)
+                blocks.append(block)
+            packets[pl.ds(k * 512 + at, 64), :] = jnp.concatenate(blocks, axis=0).astype(BF16)
+
+        @pl.when(there)
+        def _():
+            copy(k, device).start()
+
+    for k in range(10):
+        there, device, comes = links[k]
+
+        @pl.when(there)
+        def _():
+            copy(k, device).wait_send()
+
+        @pl.when(comes)
+        def _():
+            copy(k, device).wait_recv()
+
+
+def ghost_call(ghost_rows, own):
+    return pl.pallas_call(
+        ghost_kernel,
+        in_specs=[
+            pl.BlockSpec(memory_space=pltpu.SMEM),
+            pl.BlockSpec(memory_space=pltpu.VMEM),
+        ],
+        out_specs=pl.BlockSpec(memory_space=pltpu.VMEM),
+        out_shape=jax.ShapeDtypeStruct((GHOST, 128), BF16),
+        scratch_shapes=[
+            pltpu.VMEM((PARTS, 128), F32),
+            pltpu.VMEM((GHOST, 128), BF16),
+            pltpu.SemaphoreType.DMA((10,)),
+            pltpu.SemaphoreType.DMA((10,)),
+        ],
+        compiler_params=pltpu.CompilerParams(
+            collective_id=0, has_side_effects=True, vmem_limit_bytes=16 << 20
+        ),
+    )(ghost_rows, own)
+
+
+def migrant_kernel(out_ref, arrived_ref, send_sems, recv_sems):
+    links = partners(8)
+    arrived_ref[...] = jnp.zeros_like(arrived_ref)
+
+    def copy(k, device):
+        return pltpu.make_async_remote_copy(
+            src_ref=out_ref.at[k],
+            dst_ref=arrived_ref.at[k],
+            send_sem=send_sems.at[k],
+            recv_sem=recv_sems.at[k],
+            device_id=device,
+            device_id_type=MESH,
+        )
+
+    greet(links)
+    for k in (0, 2, 5, 7, 1, 6, 3, 4):
+        there, device, _ = links[k]
+
+        @pl.when(there)
+        def _():
+            copy(k, device).start()
+
+    for k in range(8):
+        there, device, comes = links[k]
+
+        @pl.when(there)
+        def _():
+            copy(k, device).wait_send()
+
+        @pl.when(comes)
+        def _():
+            copy(k, device).wait_recv()
+
+
+def migrant_call(outgoing):
+    return pl.pallas_call(
+        migrant_kernel,
+        in_specs=[pl.BlockSpec(memory_space=pltpu.VMEM)],
+        out_specs=pl.BlockSpec(memory_space=pltpu.VMEM),
+        out_shape=jax.ShapeDtypeStruct((8, MCAP, 128), BF16),
+        scratch_shapes=[pltpu.SemaphoreType.DMA((8,)), pltpu.SemaphoreType.DMA((8,))],
+        compiler_params=pltpu.CompilerParams(collective_id=1, has_side_effects=True),
+    )(outgoing)
 
 
 def per_device(
@@ -306,11 +464,7 @@
 ):
     own = latent[0]
     brick = lax.axis_index("floor").astype(jnp.int32)
-    packets = jnp.take(own, ghost_rows[0].reshape(-1), axis=0).reshape(10, 512, 128)
-    floor_blocks = shifted(packets[:8]).reshape(8 * 512, 128)
-    above = from_behind(packets[8], "slab", -1)
-    below = from_behind(packets[9], "slab", 1)
-    ext = jnp.concatenate([own, floor_blocks, above, below], axis=0)
+    ghosts = ghost_call(ghost_rows, own)
     params = (
         enc_w1,
         enc_b1.reshape(1, 128),
@@ -323,9 +477,9 @@
         node_gain.reshape(1, 128),
     )
     staying, outgoing = edge_call(
-        brick.reshape(1), edge_geom, edge_recv, own, ext, dest, edge_send, params
+        brick.reshape(1), edge_geom, edge_recv, own, ghosts, dest, edge_send, params
     )
-    arrived = shifted(outgoing.reshape(8, MCAP, 128))
+    arrived = migrant_call(outgoing.reshape(8, MCAP, 128))
     return (staying[None], arrived[None])
 
 

time: 279 us -> 173 us (0.62)
  the two profiles are of different devices: /device:TPU:30 before, /device:TPU:1 now
where the time goes in v2:
time: 173 us
  Pallas kernels  167 us (97%)
  local copies, waits for them, and re-layouts  4.94 us (3%)
    pallas_call x1, Pallas kernels, edge_call(): pl.pallas_call(edge_kernel, grid_spec=pltpu.PrefetchScalarGridSpec(num_sc...  139 us
    pallas_call x1, Pallas kernels, ghost_call(): pl.pallas_call(ghost_kernel, in_specs=[pl.BlockSpec(memory_space=pltpu.SM...  20.2 us
    pallas_call x1, Pallas kernels, migrant_call(): pl.pallas_call(migrant_kernel, in_specs=[pl.BlockSpec(memory_space=pltpu....  8.21 us
    unnamed x31, local copies, waits for them, and re-layouts  4.94 us

profile of v2, /device:TPU:1, one launch (start us, length us, event | category | flops | bytes accessed | tf_op | source)
XLA Modules:
  0.0 173.0 jit_solution(8222305016526913141)
XLA Ops:
  0.6 0.8 copy.17.rows_ref
  1.5 1.7 copy.18.geom_ref
  3.1 0.0 copy-done
  3.1 0.0 copy-start.2
  3.2 0.0 copy-start.3
  3.2 0.0 copy-start.4
  3.2 0.0 copy-start.5
  3.2 0.0 copy-start.6
  3.2 0.0 copy-start.7
  3.2 0.0 copy-start.8
  3.2 0.0 copy-start.9
  3.2 0.0 copy-start.10
  3.3 0.0 copy-start.11
  3.3 0.0 copy-start.12
  3.3 0.0 copy-start.13
  3.3 20.2 %shard_map.158.ghost_ref = bf16[5120,128]{1,0:T(8,128)(2,1)S(1)} custom-call(s32[1,10,512]{2,1,0:T(8,128)S(1)} %copy.17.rows_ref, bf16[4096,128]{1,0:T(8,128)(2,1)S(1)} %bitcast.8), custom_call_target="tpu_custom_call" | custom-call | tf_op jit(solution)/shard_map/pallas_call | solution.py:383
  23.5 0.0 copy-done.2
  23.5 0.0 copy-done.3
  23.5 0.0 copy-done.4
  23.6 138.7 %shard_map.159 = (bf16[4096,128]{1,0:T(8,128)(2,1)}, bf16[1024,128]{1,0:T(8,128)(2,1)S(1)}) custom-call(s32[1]{0:T(128)} %bitcast.brick_ref, f32[1,3,65536]{2,1,0:T(4,128)S(1)} %copy.18.geom_ref, s32[1,65536]{1,0:T(1,128)S(1)} %copy-done.2, bf16[4096,128]{1,0:T(8,128)(2,1)S(1)} %bitcast.9, bf16[4096,128]{1,0:T(8,128)(2,1)S(1)} %bitcast.10, ...), custom_call_target="tpu_custom_call" | custom-call | flops 8999999488 | bytes 6000000 | tf_op jit(solution)/shard_map/pallas_call | solution.py:234
  162.4 0.0 copy-start.1
  162.4 0.7 copy-done.1
  163.1 8.2 %shard_map.160 = bf16[8,128,128]{2,1,0:T(8,128)(2,1)} custom-call(bf16[8,128,128]{2,1,0:T(8,128)(2,1)} %bitcast.11), custom_call_target="tpu_custom_call" | custom-call | tf_op jit(solution)/shard_map/pallas_call | solution.py:438
  171.3 1.7 copy.20
  (10 shorter events, 0.0 us)
Async XLA Ops:
  0.6 2.5 %copy-start = (bf16[1,4096,128]{2,1,0:T(8,128)(2,1)S(1)}, bf16[1,4096,128]{2,1,0:T(8,128)(2,1)}, u32[]{:S(2)}) copy-start(bf16[1,4096,128]{2,1,0:T(8,128)(2,1)} %param.15) | copy-start | bytes 3145732
  3.1 20.3 %copy-start.2 = (s32[1,65536]{1,0:T(1,128)S(1)}, s32[1,65536]{1,0:T(1,128)}, u32[]{:S(2)}) copy-start(s32[1,65536]{1,0:T(1,128)} %recv_ref.1) | copy-start | bytes 786436
  3.2 20.3 %copy-start.3 = (s32[1,65536]{1,0:T(1,128)S(1)}, s32[1,65536]{1,0:T(1,128)}, u32[]{:S(2)}) copy-start(s32[1,65536]{1,0:T(1,128)} %send_hbm.1) | copy-start | bytes 786436
  3.2 20.3 %copy-start.4 = (bf16[3,128,128]{2,1,0:T(8,128)(2,1)S(1)}, bf16[3,128,128]{2,1,0:T(8,128)(2,1)}, u32[]{:S(2)}) copy-start(bf16[3,128,128]{2,1,0:T(8,128)(2,1)} %pe_w1_ref.1) | copy-start | bytes 294916
  3.2 20.3 %copy-start.5 = (bf16[2,128,128]{2,1,0:T(8,128)(2,1)S(1)}, bf16[2,128,128]{2,1,0:T(8,128)(2,1)}, u32[]{:S(2)}) copy-start(bf16[2,128,128]{2,1,0:T(8,128)(2,1)} %pn_w1_ref.1) | copy-start | bytes 196612
  3.2 20.3 %copy-start.6 = (bf16[128,128]{1,0:T(8,128)(2,1)S(1)}, bf16[128,128]{1,0:T(8,128)(2,1)}, u32[]{:S(2)}) copy-start(bf16[128,128]{1,0:T(8,128)(2,1)} %enc_w2_ref.1) | copy-start | bytes 98308
  3.2 20.3 %copy-start.7 = (bf16[128,128]{1,0:T(8,128)(2,1)S(1)}, bf16[128,128]{1,0:T(8,128)(2,1)}, u32[]{:S(2)}) copy-start(bf16[128,128]{1,0:T(8,128)(2,1)} %pe_w2_ref.1) | copy-start | bytes 98308
  3.2 20.3 %copy-start.8 = (bf16[128,128]{1,0:T(8,128)(2,1)S(1)}, bf16[128,128]{1,0:T(8,128)(2,1)}, u32[]{:S(2)}) copy-start(bf16[128,128]{1,0:T(8,128)(2,1)} %pn_w2_ref.1) | copy-start | bytes 98308
  3.2 20.3 %copy-start.9 = (s32[1,4096]{1,0:T(1,128)S(1)}, s32[1,4096]{1,0:T(1,128)}, u32[]{:S(2)}) copy-start(s32[1,4096]{1,0:T(1,128)} %dest_ref.1) | copy-start | bytes 49156
  3.2 20.3 %copy-start.10 = (f32[4,128]{1,0:T(4,128)S(1)}, f32[4,128]{1,0:T(4,128)}, u32[]{:S(2)}) copy-start(f32[4,128]{1,0:T(4,128)} %enc_w1_ref.1) | copy-start | bytes 6148
  3.3 20.3 %copy-start.11 = (f32[128]{0:T(128)S(1)}, f32[128]{0:T(128)}, u32[]{:S(2)}) copy-start(f32[128]{0:T(128)} %param.22) | copy-start | bytes 1540
  3.3 20.3 %copy-start.12 = (f32[128]{0:T(128)S(1)}, f32[128]{0:T(128)}, u32[]{:S(2)}) copy-start(f32[128]{0:T(128)} %param.26) | copy-start | bytes 1540
  3.3 20.3 %copy-start.13 = (f32[128]{0:T(128)S(1)}, f32[128]{0:T(128)}, u32[]{:S(2)}) copy-start(f32[128]{0:T(128)} %param.29) | copy-start | bytes 1540
  162.4 0.7 copy-start.1

commit v3 on v2

v3 whole, which is shorter than its diff:
```python
import jax
import jax.numpy as jnp
from jax import lax
from jax.experimental import pallas as pl
from jax.experimental.pallas import tpu as pltpu
from jax.sharding import PartitionSpec as P

BCOLS = 4
MCAP = 128
TILE = 128
TILES = 32
CHUNK = 1024
PAIR = 512
PER = 2048 // CHUNK
BLOCK = 512
PARTS = 4096
GHOST = 5120
STEP_ROW = (-1, -1, -1, 0, 0, 1, 1, 1)
STEP_COL = (-1, 0, 1, -1, 1, -1, 0, 1)
EPS = 1e-05
F32 = jnp.float32
BF16 = jnp.bfloat16


def dot(a, b):
    return jnp.dot(a, b, preferred_element_type=F32)


def iota(shape, dim):
    return lax.broadcasted_iota(jnp.int32, shape, dim)


def edge_kernel(
    brick_ref,
    geom_ref,
    recv_ref,
    own_ref,
    ghost_ref,
    dest_ref,
    send_hbm,
    enc_w1_ref,
    enc_b1_ref,
    enc_w2_ref,
    pe_w1_ref,
    pe_w2_ref,
    edge_gain_ref,
    pn_w1_ref,
    pn_w2_ref,
    node_gain_ref,
    staying_ref,
    outgoing_ref,
    table,
    recv_proj,
    summed,
    w_first,
    w_enc,
    w_msg,
    w_node,
    hidden,
    picked,
    picked_t,
    encoded,
    mixed,
    message,
    counts,
    updated,
    leaving,
    send_0,
    send_1,
    send_2,
    send_3,
    sems,
):
    slots = (send_0, send_1, send_2, send_3)
    chunks = TILES * PER

    def fetch(slot, chunk):
        at = jnp.clip(chunk, 0, chunks - 1) * CHUNK
        return pltpu.make_async_copy(
            send_hbm.at[:, pl.ds(pl.multiple_of(at, CHUNK), CHUNK)], slots[slot], sems.at[slot]
        )

    for ahead in (-2, -1, 0):
        fetch(ahead % 4, ahead).start()

    w_first[...] = jnp.zeros_like(w_first)
    w_enc[...] = jnp.zeros_like(w_enc)
    w_msg[...] = jnp.zeros_like(w_msg)
    counts[...] = jnp.zeros_like(counts)
    leaving[...] = jnp.zeros_like(leaving)
    row8 = iota((8, 128), 0)
    weights = jnp.zeros((8, 128), F32)
    for c in range(4):
        weights = jnp.where(row8 == c, enc_w1_ref[c : c + 1, :], weights)
    weights = jnp.where(row8 == 4, enc_b1_ref[0:1, :], weights)
    high = weights.astype(BF16).astype(F32)
    weights = jnp.concatenate(
        [high, high, weights - high, jnp.zeros((8, 128), F32)], axis=0
    ).astype(BF16)
    w_first[0:32, 0:128] = weights
    w_first[32:64, 128:256] = weights

    def centred(ref):
        full = ref[...].astype(F32)
        return full - jnp.mean(full, axis=1, keepdims=True)

    enc = centred(enc_w2_ref).astype(BF16)
    msg = centred(pe_w2_ref).astype(BF16)
    for k in (0, 128):
        w_enc[k : k + 128, k : k + 128] = enc
        w_msg[k : k + 128, k : k + 128] = msg
    full = centred(pn_w2_ref)
    high = full.astype(BF16)
    w_node[0:128, :] = high
    w_node[128:256, :] = (full - high.astype(F32)).astype(BF16)

    w_both = jnp.concatenate([pe_w1_ref[2], pe_w1_ref[1]], axis=1)

    @pl.loop(0, PARTS // 1024)
    def _(i):
        at = pl.multiple_of(i * 1024, 1024)
        block = dot(own_ref[pl.ds(at, 1024), :], w_both).astype(BF16)
        table[pl.ds(at, 1024), :] = block[:, 0:128].astype(F32)
        recv_proj[pl.ds(at, 1024), :] = block[:, 128:256]

    @pl.loop(0, GHOST // 1024)
    def _(i):
        at = pl.multiple_of(i * 1024, 1024)
        block = dot(ghost_ref[pl.ds(at, 1024), :], pe_w1_ref[2])
        table[pl.ds(PARTS + at, 1024), :] = block.astype(BF16).astype(F32)

    rows = iota((TILE, CHUNK), 0)
    r8 = iota((8, CHUNK), 0)

    def gathered(slot, first, count):
        blocks = []
        for at in range(first, first + count, 8):
            block = jnp.broadcast_to(table[pl.ds(slot[0, at], 1), :], (8, 128))
            for s in range(1, 8):
                line = jnp.broadcast_to(table[pl.ds(slot[0, at + s], 1), :], (8, 128))
                block = jnp.where(row8 == s, line, block)
            blocks.append(block)
        return jnp.concatenate(blocks, axis=0)

    def normed(values):
        spread = jnp.sum(values * values, axis=1, keepdims=True) * (1.0 / 128)
        return (values * lax.rsqrt(spread + EPS)).astype(BF16)

    def first_layer(chunk, tile, q):
        at = pl.multiple_of(chunk * CHUNK, CHUNK)
        geom = geom_ref[0, :, pl.ds(at, CHUNK)]
        local = recv_ref[:, pl.ds(at, CHUNK)] - tile * TILE
        length = jnp.sqrt(geom[0:1] * geom[0:1] + geom[1:2] * geom[1:2] + geom[2:3] * geom[2:3])
        feats = jnp.where(r8 == 4, 1.0, jnp.zeros((8, CHUNK), F32))
        for c in range(3):
            feats = jnp.where(r8 == c, geom[c : c + 1], feats)
        feats = jnp.where(r8 == 3, length, feats)
        high = feats.astype(BF16).astype(F32)
        low = feats - high
        feats = jnp.concatenate([high, low, high, jnp.zeros_like(high)], axis=0)
        feats = jnp.concatenate([feats[:, 0:PAIR], feats[:, PAIR:CHUNK]], axis=0).astype(BF16)
        out = lax.dot_general(
            feats, w_first[...], (((0,), (0,)), ((), ())), preferred_element_type=F32
        )
        hidden[...] = jnp.maximum(out, 0.0).astype(BF16)
        picks_t = jnp.where(rows == local, 1.0, 0.0).astype(BF16)
        picked_t[q] = picks_t
        picked[q % 2] = picks_t.T

    def encode(q):
        out = dot(hidden[...], w_enc[...])
        encoded[q, :, 0:128] = normed(out[:, 0:128])
        encoded[q, :, 128:256] = normed(out[:, 128:256])

    def mix(tile, q):
        at = pl.multiple_of(tile * TILE, TILE)
        w_mix = jnp.concatenate([pe_w1_ref[0], recv_proj[pl.ds(at, TILE), :]], axis=0)
        for side in range(2):
            lanes = slice(side * 128, side * 128 + 128)
            lhs = jnp.concatenate(
                [encoded[q, :, lanes], picked[q % 2, side * PAIR : side * PAIR + PAIR, :]], axis=1
            )
            out = dot(lhs, w_mix) + gathered(slots[q], side * PAIR, PAIR)
            mixed[:, lanes] = jnp.maximum(out, 0.0).astype(BF16)

    def messages():
        out = dot(mixed[...], w_msg[...])
        message[:, 0:128] = normed(out[:, 0:128])
        message[:, 128:256] = normed(out[:, 128:256])

    def gather_up(tile, q, first):
        out = None
        for side in range(2):
            lanes = slice(side * 128, side * 128 + 128)
            rhs = jnp.concatenate([encoded[q, :, lanes], message[:, lanes]], axis=1)
            part = dot(picked_t[q, :, side * PAIR : side * PAIR + PAIR], rhs)
            out = part if side == 0 else out + part
        at = pl.multiple_of(tile * TILE, TILE)
        if first:
            summed[pl.ds(at, TILE), :] = out
        else:
            summed[pl.ds(at, TILE), :] += out

    def body(t, q, final=False):
        chunk = t * 4 + q

        def tile(back):
            at = t * (4 // PER) + (q - back) // PER
            return at if final else jnp.maximum(at, 0)

        live = lambda back: not final or q < back
        if live(2):
            fetch((q - 2) % 4, chunk - 2).wait()
        if live(-1):
            fetch((q + 1) % 4, chunk + 1).start()
        gather_up(tile(4), q, q % PER == 0)
        if live(3):
            messages()
        if live(2):
            mix(tile(2), (q - 2) % 4)
        if live(1):
            encode((q - 1) % 4)
        if live(0):
            first_layer(chunk, tile(0), q)

    @pl.loop(0, chunks // 4)
    def _(t):
        for q in range(4):
            body(t, q)

    for q in range(4):
        body(chunks // 4, q, True)
    fetch(0, chunks).wait()

    brick = brick_ref[0]
    k8 = iota((8, TILE), 0)
    k9 = jnp.where(k8 >= 4, k8 + 1, k8)
    diagonal = iota((TILE, TILE), 0) == iota((TILE, TILE), 1)
    upper = jnp.where(iota((TILE, TILE), 0) <= iota((TILE, TILE), 1), 1.0, 0.0).astype(BF16)

    w_both = jnp.concatenate([pn_w1_ref[0], pn_w1_ref[1]], axis=0)

    def node(b):
        at = pl.multiple_of(b * BLOCK, BLOCK)
        own = own_ref[pl.ds(at, BLOCK), :]
        total = summed[pl.ds(at, BLOCK), :]
        aggregate = (total[:, 0:128] + edge_gain_ref[0:1, :] * total[:, 128:256]).astype(BF16)
        out = dot(jnp.concatenate([own, aggregate], axis=1), w_both)
        out = jnp.maximum(out, 0.0).astype(BF16)
        out = dot(jnp.concatenate([out, out], axis=1), w_node[...])
        spread = jnp.sum(out * out, axis=1, keepdims=True) * (1.0 / 128)
        out = out * lax.rsqrt(spread + EPS)
        fresh = (own.astype(F32) + node_gain_ref[0:1, :] * out).astype(BF16)
        updated[pl.ds(at, BLOCK), :] = fresh
        for i in range(0, BLOCK, TILE):
            dest = dest_ref[:, pl.ds(at + i, TILE)]
            stays = jnp.where(diagonal & (dest == brick), 1.0, 0.0).astype(BF16)
            staying_ref[pl.ds(at + i, TILE), :] = dot(stays, fresh[i : i + TILE]).astype(BF16)

    def pack(b):
        at = pl.multiple_of(b * BLOCK, BLOCK)
        places = []
        seen = counts[...]
        for i in range(0, BLOCK, TILE):
            dest = dest_ref[:, pl.ds(at + i, TILE)]
            move_row = dest // BCOLS - brick // BCOLS
            move_col = dest % BCOLS - brick % BCOLS
            code = (move_row + 1) * 3 + move_col + 1
            heads = jnp.where(code == k9, 1.0, 0.0)
            running = dot(heads.astype(BF16), upper) + seen
            seen = seen + jnp.sum(heads, axis=1, keepdims=True)
            places.append(
                jnp.sum(
                    heads * (running + (k8 * MCAP).astype(F32)), axis=0, keepdims=True
                ).astype(jnp.int32) - 1
            )
        counts[...] = seen
        place = jnp.concatenate(places, axis=1)
        for k in range(0, 8 * MCAP, 256):
            chosen = jnp.where(iota((256, BLOCK), 0) + k == place, 1.0, 0.0).astype(BF16)
            leaving[k : k + 256, :] += dot(chosen, updated[pl.ds(at, BLOCK), :])

    node(0)

    @pl.loop(1, PARTS // BLOCK)
    def _(b):
        pack(b - 1)
        node(b)

    pack(PARTS // BLOCK - 1)
    outgoing_ref[...] = leaving[...].astype(BF16)


def edge_call(brick, geom, recv, own, ghosts, dest, send, params):
    vmem = pl.BlockSpec(memory_space=pltpu.VMEM)
    return pl.pallas_call(
        edge_kernel,
        in_specs=[pl.BlockSpec(memory_space=pltpu.SMEM)]
        + [vmem] * 5
        + [pl.BlockSpec(memory_space=pl.ANY)]
        + [vmem] * 9,
        out_specs=[vmem, vmem],
        out_shape=[
            jax.ShapeDtypeStruct((PARTS, 128), BF16),
            jax.ShapeDtypeStruct((8 * MCAP, 128), BF16),
        ],
        scratch_shapes=[
            pltpu.VMEM((PARTS + GHOST, 128), F32),
            pltpu.VMEM((PARTS, 128), BF16),
            pltpu.VMEM((PARTS, 256), F32),
            pltpu.VMEM((64, 256), BF16),
            pltpu.VMEM((256, 256), BF16),
            pltpu.VMEM((256, 256), BF16),
            pltpu.VMEM((256, 128), BF16),
            pltpu.VMEM((PAIR, 256), BF16),
            pltpu.VMEM((2, CHUNK, 128), BF16),
            pltpu.VMEM((4, TILE, CHUNK), BF16),
            pltpu.VMEM((4, PAIR, 256), BF16),
            pltpu.VMEM((PAIR, 256), BF16),
            pltpu.VMEM((PAIR, 256), BF16),
            pltpu.VMEM((8, 128), F32),
            pltpu.VMEM((PARTS, 128), BF16),
            pltpu.VMEM((8 * MCAP, 128), F32),
        ]
        + [pltpu.SMEM((1, CHUNK), jnp.int32)] * 4
        + [pltpu.SemaphoreType.DMA((4,))],
        compiler_params=pltpu.CompilerParams(vmem_limit_bytes=40 << 20),
        cost_estimate=pl.CostEstimate(
            flops=9_000_000_000, bytes_accessed=6_000_000, transcendentals=1_000_000
        ),
    )(brick, geom, recv, own, ghosts, dest, send, *params)


MESH = pl.DeviceIdType.MESH


def partners(count):
    floor, slab = lax.axis_index("floor"), lax.axis_index("slab")
    row, col = floor // BCOLS, floor % BCOLS
    rows = lax.axis_size("floor") // BCOLS
    slabs = lax.axis_size("slab")

    def inside(r, c):
        return (r >= 0) & (r < rows) & (c >= 0) & (c < BCOLS)

    found = []
    for dr, dc in zip(STEP_ROW, STEP_COL):
        found.append(
            (
                inside(row + dr, col + dc),
                (floor + dr * BCOLS + dc, slab),
                inside(row - dr, col - dc),
            )
        )
    found.append((slab >= 1, (floor, slab - 1), slab + 1 < slabs))
    found.append((slab + 1 < slabs, (floor, slab + 1), slab >= 1))
    return found[:count]


def greet(links):
    barrier = pltpu.get_barrier_semaphore()
    for there, device, _ in links:

        @pl.when(there)
        def _():
            pl.semaphore_signal(barrier, inc=1, device_id=device, device_id_type=MESH)

    peers = 0
    for there, _, _ in links:
        peers = peers + there.astype(jnp.int32)
    pl.semaphore_wait(barrier, peers)


def ghost_kernel(rows_ref, own_ref, ghost_ref, table, packets, send_sems, recv_sems):
    links = partners(10)
    row8 = iota((8, 128), 0)
    ghost_ref[...] = jnp.zeros_like(ghost_ref)

    @pl.loop(0, PARTS // 256)
    def _(i):
        at = pl.multiple_of(i * 256, 256)
        table[pl.ds(at, 256), :] = own_ref[pl.ds(at, 256), :].astype(F32)

    def copy(k, device):
        block = pl.ds(k * 512, 512)
        return pltpu.make_async_remote_copy(
            src_ref=packets.at[block],
            dst_ref=ghost_ref.at[block],
            send_sem=send_sems.at[k],
            recv_sem=recv_sems.at[k],
            device_id=device,
            device_id_type=MESH,
        )

    greet(links)
    for k in (0, 2, 5, 7, 1, 6, 3, 4, 8, 9):
        there, device, _ = links[k]

        @pl.loop(0, 8)
        def _(c):
            at = pl.multiple_of(c * 64, 64)
            blocks = []
            for first in range(0, 64, 8):
                block = None
                for s in range(8):
                    line = jnp.broadcast_to(
                        table[pl.ds(rows_ref[0, k, at + first + s], 1), :], (8, 128)
                    )
                    block = line if s == 0 else jnp.where(row8 == s, line, block)
                blocks.append(block)
            packets[pl.ds(k * 512 + at, 64), :] = jnp.concatenate(blocks, axis=0).astype(BF16)

        @pl.when(there)
        def _():
            copy(k, device).start()

    for k in range(10):
        there, device, comes = links[k]

        @pl.when(there)
        def _():
            copy(k, device).wait_send()

        @pl.when(comes)
        def _():
            copy(k, device).wait_recv()


def ghost_call(ghost_rows, own):
    return pl.pallas_call(
        ghost_kernel,
        in_specs=[
            pl.BlockSpec(memory_space=pltpu.SMEM),
            pl.BlockSpec(memory_space=pltpu.VMEM),
        ],
        out_specs=pl.BlockSpec(memory_space=pltpu.VMEM),
        out_shape=jax.ShapeDtypeStruct((GHOST, 128), BF16),
        scratch_shapes=[
            pltpu.VMEM((PARTS, 128), F32),
            pltpu.VMEM((GHOST, 128), BF16),
            pltpu.SemaphoreType.DMA((10,)),
            pltpu.SemaphoreType.DMA((10,)),
        ],
        compiler_params=pltpu.CompilerParams(
            collective_id=0, has_side_effects=True, vmem_limit_bytes=16 << 20
        ),
    )(ghost_rows, own)


def migrant_kernel(out_ref, arrived_ref, send_sems, recv_sems):
    links = partners(8)
    arrived_ref[...] = jnp.zeros_like(arrived_ref)

    def copy(k, device):
        return pltpu.make_async_remote_copy(
            src_ref=out_ref.at[k],
            dst_ref=arrived_ref.at[k],
            send_sem=send_sems.at[k],
            recv_sem=recv_sems.at[k],
            device_id=device,
            device_id_type=MESH,
        )

    greet(links)
    for k in (0, 2, 5, 7, 1, 6, 3, 4):
        there, device, _ = links[k]

        @pl.when(there)
        def _():
            copy(k, device).start()

    for k in range(8):
        there, device, comes = links[k]

        @pl.when(there)
        def _():
            copy(k, device).wait_send()

        @pl.when(comes)
        def _():
            copy(k, device).wait_recv()


def migrant_call(outgoing):
    return pl.pallas_call(
        migrant_kernel,
        in_specs=[pl.BlockSpec(memory_space=pltpu.VMEM)],
        out_specs=pl.BlockSpec(memory_space=pltpu.VMEM),
        out_shape=jax.ShapeDtypeStruct((8, MCAP, 128), BF16),
        scratch_shapes=[pltpu.SemaphoreType.DMA((8,)), pltpu.SemaphoreType.DMA((8,))],
        compiler_params=pltpu.CompilerParams(collective_id=1, has_side_effects=True),
    )(outgoing)


def per_device(
    latent,
    edge_geom,
    edge_recv,
    edge_send,
    ghost_rows,
    dest,
    enc_w1,
    enc_b1,
    enc_w2,
    pe_w1,
    pe_w2,
    edge_gain,
    pn_w1,
    pn_w2,
    node_gain,
):
    own = latent[0]
    brick = lax.axis_index("floor").astype(jnp.int32)
    ghosts = ghost_call(ghost_rows, own)
    params = (
        enc_w1,
        enc_b1.reshape(1, 128),
        enc_w2,
        pe_w1,
        pe_w2,
        edge_gain.reshape(1, 128),
        pn_w1,
        pn_w2,
        node_gain.reshape(1, 128),
    )
    staying, outgoing = edge_call(
        brick.reshape(1), edge_geom, edge_recv, own, ghosts, dest, edge_send, params
    )
    arrived = migrant_call(outgoing.reshape(8, MCAP, 128))
    return (staying[None], arrived[None])


def solution(mesh):
    in_specs = (
        P("slab", "floor", None),
        P("slab", None, "floor"),
        P("slab", "floor"),
        P("slab", "floor"),
        P("slab", "floor", None),
        P("slab", "floor"),
    ) + (P(),) * 9
    out_specs = (P("slab", "floor", None), P("slab", "floor", None, None))
    return jax.shard_map(
        per_device, mesh=mesh, in_specs=in_specs, out_specs=out_specs, check_vma=False
    )
```

time: 173 us -> 118 us (0.68)
  Pallas kernels: 167 us -> 112 us
    pallas_call x1, Pallas kernels: 139 us -> 84 us  [edge_call(): pl.pallas_call(edge_kernel, in_specs=[pl.BlockSpec(memory_space=pltpu.SME...]
where the time goes in v3:
time: 118 us
  Pallas kernels  112 us (95%)
  local copies, waits for them, and re-layouts  4.94 us (4%)
    pallas_call x1, Pallas kernels, edge_call(): pl.pallas_call(edge_kernel, in_specs=[pl.BlockSpec(memory_space=pltpu.SME...  84 us
    pallas_call x1, Pallas kernels, ghost_call(): pl.pallas_call(ghost_kernel, in_specs=[pl.BlockSpec(memory_space=pltpu.SM...  20.2 us
    pallas_call x1, Pallas kernels, migrant_call(): pl.pallas_call(migrant_kernel, in_specs=[pl.BlockSpec(memory_space=pltpu....  8.23 us
    unnamed x31, local copies, waits for them, and re-layouts  4.94 us

profile of v3, /device:TPU:1, one launch (start us, length us, event | category | flops | bytes accessed | tf_op | source)
XLA Modules:
  0.0 118.3 jit_solution(10569223921996477724)
XLA Ops:
  0.6 0.8 copy.17.rows_ref
  1.5 1.7 %copy.18.geom_ref = f32[1,3,65536]{2,1,0:T(4,128)S(1)} copy(f32[1,3,65536]{2,0,1:T(1,128)} %param.16) | data formatting | bytes 1572864 | tf_op args[1]
  3.1 0.0 copy-done
  3.1 0.0 copy-start.2
  3.2 0.0 copy-start.3
  3.2 0.0 copy-start.4
  3.2 0.0 copy-start.5
  3.2 0.0 copy-start.6
  3.2 0.0 copy-start.7
  3.2 0.0 copy-start.8
  3.2 0.0 copy-start.9
  3.2 0.0 copy-start.10
  3.3 0.0 copy-start.11
  3.3 0.0 copy-start.12
  3.3 0.0 copy-start.13
  3.3 20.2 %shard_map.158.ghost_ref = bf16[5120,128]{1,0:T(8,128)(2,1)S(1)} custom-call(s32[1,10,512]{2,1,0:T(8,128)S(1)} %copy.17.rows_ref, bf16[4096,128]{1,0:T(8,128)(2,1)S(1)} %bitcast.8), custom_call_target="tpu_custom_call" | custom-call | tf_op jit(solution)/shard_map/pallas_call | solution.py:430
  23.5 0.0 copy-done.2
  23.5 0.0 copy-done.3
  23.5 0.0 copy-done.4
  23.6 84.0 %shard_map.159 = (bf16[4096,128]{1,0:T(8,128)(2,1)}, bf16[1024,128]{1,0:T(8,128)(2,1)S(1)}) custom-call(s32[1]{0:T(128)} %bitcast.brick_ref, f32[1,3,65536]{2,1,0:T(4,128)S(1)} %copy.18.geom_ref, s32[1,65536]{1,0:T(1,128)S(1)} %copy-done.2, bf16[4096,128]{1,0:T(8,128)(2,1)S(1)} %bitcast.9, bf16[5120,128]{1,0:T(8,128)(2,1)S(1)} %shard_map.158.ghost_ref, ...), custom_call_target="tpu_custom_call" | custom-call | flops 8999999488 | bytes 6000000 | tf_op jit(solution)/shard_map/pallas_call | solution.py:296
  107.6 0.0 copy-start.1
  107.7 0.7 copy-done.1
  108.3 8.2 %shard_map.160 = bf16[8,128,128]{2,1,0:T(8,128)(2,1)} custom-call(bf16[8,128,128]{2,1,0:T(8,128)(2,1)} %bitcast.10), custom_call_target="tpu_custom_call" | custom-call | tf_op jit(solution)/shard_map/pallas_call | solution.py:485
  116.6 1.7 %copy.20 = bf16[1,8,128,128]{3,2,1,0:T(8,128)(2,1)} copy(bf16[1,8,128,128]{3,2,1,0:T(8,128)(2,1)} %bitcast.14) | data formatting | bytes 524288
  (10 shorter events, 0.0 us)
Async XLA Ops:
  0.6 2.5 %copy-start = (bf16[1,4096,128]{2,1,0:T(8,128)(2,1)S(1)}, bf16[1,4096,128]{2,1,0:T(8,128)(2,1)}, u32[]{:S(2)}) copy-start(bf16[1,4096,128]{2,1,0:T(8,128)(2,1)} %param.15) | copy-start | bytes 3145732
  3.1 20.3 %copy-start.2 = (s32[1,65536]{1,0:T(1,128)S(1)}, s32[1,65536]{1,0:T(1,128)}, u32[]{:S(2)}) copy-start(s32[1,65536]{1,0:T(1,128)} %recv_ref.1) | copy-start | bytes 786436
  3.2 20.3 %copy-start.3 = (s32[1,65536]{1,0:T(1,128)S(1)}, s32[1,65536]{1,0:T(1,128)}, u32[]{:S(2)}) copy-start(s32[1,65536]{1,0:T(1,128)} %send_hbm.1) | copy-start | bytes 786436
  3.2 20.3 %copy-start.4 = (bf16[3,128,128]{2,1,0:T(8,128)(2,1)S(1)}, bf16[3,128,128]{2,1,0:T(8,128)(2,1)}, u32[]{:S(2)}) copy-start(bf16[3,128,128]{2,1,0:T(8,128)(2,1)} %pe_w1_ref.1) | copy-start | bytes 294916
  3.2 20.3 %copy-start.5 = (bf16[2,128,128]{2,1,0:T(8,128)(2,1)S(1)}, bf16[2,128,128]{2,1,0:T(8,128)(2,1)}, u32[]{:S(2)}) copy-start(bf16[2,128,128]{2,1,0:T(8,128)(2,1)} %pn_w1_ref.1) | copy-start | bytes 196612
  3.2 20.3 %copy-start.6 = (bf16[128,128]{1,0:T(8,128)(2,1)S(1)}, bf16[128,128]{1,0:T(8,128)(2,1)}, u32[]{:S(2)}) copy-start(bf16[128,128]{1,0:T(8,128)(2,1)} %enc_w2_ref.1) | copy-start | bytes 98308
  3.2 20.3 %copy-start.7 = (bf16[128,128]{1,0:T(8,128)(2,1)S(1)}, bf16[128,128]{1,0:T(8,128)(2,1)}, u32[]{:S(2)}) copy-start(bf16[128,128]{1,0:T(8,128)(2,1)} %pe_w2_ref.1) | copy-start | bytes 98308
  3.2 20.3 %copy-start.8 = (bf16[128,128]{1,0:T(8,128)(2,1)S(1)}, bf16[128,128]{1,0:T(8,128)(2,1)}, u32[]{:S(2)}) copy-start(bf16[128,128]{1,0:T(8,128)(2,1)} %pn_w2_ref.1) | copy-start | bytes 98308
  3.2 20.3 %copy-start.9 = (s32[1,4096]{1,0:T(1,128)S(1)}, s32[1,4096]{1,0:T(1,128)}, u32[]{:S(2)}) copy-start(s32[1,4096]{1,0:T(1,128)} %dest_ref.1) | copy-start | bytes 49156
  3.2 20.3 %copy-start.10 = (f32[4,128]{1,0:T(4,128)S(1)}, f32[4,128]{1,0:T(4,128)}, u32[]{:S(2)}) copy-start(f32[4,128]{1,0:T(4,128)} %enc_w1_ref.1) | copy-start | bytes 6148
  3.3 20.3 %copy-start.11 = (f32[128]{0:T(128)S(1)}, f32[128]{0:T(128)}, u32[]{:S(2)}) copy-start(f32[128]{0:T(128)} %param.22) | copy-start | bytes 1540
  3.3 20.3 %copy-start.12 = (f32[128]{0:T(128)S(1)}, f32[128]{0:T(128)}, u32[]{:S(2)}) copy-start(f32[128]{0:T(128)} %param.26) | copy-start | bytes 1540
  3.3 20.3 %copy-start.13 = (f32[128]{0:T(128)S(1)}, f32[128]{0:T(128)}, u32[]{:S(2)}) copy-start(f32[128]{0:T(128)} %param.29) | copy-start | bytes 1540
  107.6 0.7 copy-start.1

commit v4 on v3

--- a/solution.py
+++ b/solution.py
@@ -12,7 +12,7 @@
 CHUNK = 1024
 PAIR = 512
 PER = 2048 // CHUNK
-BLOCK = 512
+BLOCK = 1024
 PARTS = 4096
 GHOST = 5120
 STEP_ROW = (-1, -1, -1, 0, 0, 1, 1, 1)
@@ -56,6 +56,7 @@
     w_enc,
     w_msg,
     w_node,
+    w_mean,
     hidden,
     picked,
     picked_t,
@@ -85,6 +86,7 @@
 
     w_first[...] = jnp.zeros_like(w_first)
     w_enc[...] = jnp.zeros_like(w_enc)
+    w_mean[...] = jnp.zeros_like(w_mean)
     w_msg[...] = jnp.zeros_like(w_msg)
     counts[...] = jnp.zeros_like(counts)
     leaving[...] = jnp.zeros_like(leaving)
@@ -108,6 +110,7 @@
     msg = centred(pe_w2_ref).astype(BF16)
     for k in (0, 128):
         w_enc[k : k + 128, k : k + 128] = enc
+        w_mean[k : k + 128, k : k + 128] = jnp.full((128, 128), 1.0 / 128, BF16)
         w_msg[k : k + 128, k : k + 128] = msg
     full = centred(pn_w2_ref)
     high = full.astype(BF16)
@@ -116,14 +119,14 @@
 
     w_both = jnp.concatenate([pe_w1_ref[2], pe_w1_ref[1]], axis=1)
 
-    @pl.loop(0, PARTS // 1024)
+    @pl.loop(0, PARTS // 1024, unroll=2)
     def _(i):
         at = pl.multiple_of(i * 1024, 1024)
         block = dot(own_ref[pl.ds(at, 1024), :], w_both).astype(BF16)
         table[pl.ds(at, 1024), :] = block[:, 0:128].astype(F32)
         recv_proj[pl.ds(at, 1024), :] = block[:, 128:256]
 
-    @pl.loop(0, GHOST // 1024)
+    @pl.loop(0, GHOST // 1024, unroll=True)
     def _(i):
         at = pl.multiple_of(i * 1024, 1024)
         block = dot(ghost_ref[pl.ds(at, 1024), :], pe_w1_ref[2])
@@ -144,6 +147,11 @@
 
     def normed(values):
         spread = jnp.sum(values * values, axis=1, keepdims=True) * (1.0 / 128)
+        return (values * lax.rsqrt(spread + EPS)).astype(BF16)
+
+    def normed_pair(values):
+        half = values.astype(BF16)
+        spread = dot(half * half, w_mean[...])
         return (values * lax.rsqrt(spread + EPS)).astype(BF16)
 
     def first_layer(chunk, tile, q):
@@ -169,8 +177,7 @@
 
     def encode(q):
         out = dot(hidden[...], w_enc[...])
-        encoded[q, :, 0:128] = normed(out[:, 0:128])
-        encoded[q, :, 128:256] = normed(out[:, 128:256])
+        encoded[q] = normed_pair(out)
 
     def mix(tile, q):
         at = pl.multiple_of(tile * TILE, TILE)
@@ -185,8 +192,7 @@
 
     def messages():
         out = dot(mixed[...], w_msg[...])
-        message[:, 0:128] = normed(out[:, 0:128])
-        message[:, 128:256] = normed(out[:, 128:256])
+        message[...] = normed_pair(out)
 
     def gather_up(tile, q, first):
         out = None
@@ -312,6 +318,7 @@
             pltpu.VMEM((256, 256), BF16),
             pltpu.VMEM((256, 256), BF16),
             pltpu.VMEM((256, 128), BF16),
+            pltpu.VMEM((256, 256), BF16),
             pltpu.VMEM((PAIR, 256), BF16),
             pltpu.VMEM((2, CHUNK, 128), BF16),
             pltpu.VMEM((4, TILE, CHUNK), BF16),
@@ -365,6 +372,9 @@
         def _():
             pl.semaphore_signal(barrier, inc=1, device_id=device, device_id_type=MESH)
 
+
+def answered(links):
+    barrier = pltpu.get_barrier_semaphore()
     peers = 0
     for there, _, _ in links:
         peers = peers + there.astype(jnp.int32)
@@ -375,6 +385,7 @@
     links = partners(10)
     row8 = iota((8, 128), 0)
     ghost_ref[...] = jnp.zeros_like(ghost_ref)
+    greet(links)
 
     @pl.loop(0, PARTS // 256)
     def _(i):
@@ -392,15 +403,14 @@
             device_id_type=MESH,
         )
 
-    greet(links)
     for k in (0, 2, 5, 7, 1, 6, 3, 4, 8, 9):
         there, device, _ = links[k]
 
-        @pl.loop(0, 8)
+        @pl.loop(0, 4)
         def _(c):
-            at = pl.multiple_of(c * 64, 64)
+            at = pl.multiple_of(c * 128, 128)
             blocks = []
-            for first in range(0, 64, 8):
+            for first in range(0, 128, 8):
                 block = None
                 for s in range(8):
                     line = jnp.broadcast_to(
@@ -408,7 +418,10 @@
                     )
                     block = line if s == 0 else jnp.where(row8 == s, line, block)
                 blocks.append(block)
-            packets[pl.ds(k * 512 + at, 64), :] = jnp.concatenate(blocks, axis=0).astype(BF16)
+            packets[pl.ds(k * 512 + at, 128), :] = jnp.concatenate(blocks, axis=0).astype(BF16)
+
+        if k == 0:
+            answered(links)
 
         @pl.when(there)
         def _():
@@ -462,6 +475,7 @@
         )
 
     greet(links)
+    answered(links)
     for k in (0, 2, 5, 7, 1, 6, 3, 4):
         there, device, _ = links[k]
 
@@ -527,6 +541,8 @@
         brick.reshape(1), edge_geom, edge_recv, own, ghosts, dest, edge_send, params
     )
     arrived = migrant_call(outgoing.reshape(8, MCAP, 128))
+    present = jnp.stack([comes for _, _, comes in partners(8)])
+    arrived = jnp.where(present[:, None, None], arrived, jnp.zeros_like(arrived))
     return (staying[None], arrived[None])
 
 

time: 118 us -> 111 us (0.941)
  Pallas kernels: 112 us -> 106 us
  local copies, waits for them, and re-layouts: 4.94 us -> 2.66 us
  other arithmetic: 0 us -> 1.74 us
    pallas_call x1, Pallas kernels: 84 us -> 78.7 us  [edge_call(): pl.pallas_call(edge_kernel, in_specs=[pl.BlockSpec(memory_space=pltpu.SME...]
    unnamed x31 -> x32, local copies, waits for them, and re-layouts: 4.94 us -> 2.55 us
    broadcast_in_dim x0 -> x1, other arithmetic: none -> 1.74 us  [per_device(): return (staying[None], arrived[None])]
    pallas_call x1, Pallas kernels: 20.2 us -> 18.6 us  [ghost_call(): pl.pallas_call(ghost_kernel, in_specs=[pl.BlockSpec(memory_space=pltpu.SM...]
where the time goes in v4:
time: 111 us
  Pallas kernels  106 us (95%)
  local copies, waits for them, and re-layouts  2.66 us (2%)
  other arithmetic  1.74 us (2%)
    pallas_call x1, Pallas kernels, edge_call(): pl.pallas_call(edge_kernel, in_specs=[pl.BlockSpec(memory_space=pltpu.SME...  78.7 us
    pallas_call x1, Pallas kernels, ghost_call(): pl.pallas_call(ghost_kernel, in_specs=[pl.BlockSpec(memory_space=pltpu.SM...  18.6 us
    pallas_call x1, Pallas kernels, migrant_call(): pl.pallas_call(migrant_kernel, in_specs=[pl.BlockSpec(memory_space=pltpu....  8.24 us
    unnamed x32, local copies, waits for them, and re-layouts  2.55 us

profile of v4, /device:TPU:1, one launch (start us, length us, event | category | flops | bytes accessed | tf_op | source)
XLA Modules:
  0.0 111.0 jit_solution(12553880367326056918)
XLA Ops:
  0.6 0.0 copy-start
  0.6 0.0 copy-start.14
  0.7 1.8 %copy.18.geom_ref = f32[1,3,65536]{2,1,0:T(4,128)S(1)} copy(f32[1,3,65536]{2,0,1:T(1,128)} %param.16) | data formatting | bytes 1572864 | tf_op args[1]
  2.4 0.0 copy-start.2
  2.4 0.0 copy-start.3
  2.4 0.0 copy-start.4
  2.5 0.0 copy-start.5
  2.5 0.0 copy-start.6
  2.5 0.0 copy-start.7
  2.5 0.0 copy-start.8
  2.5 0.0 copy-start.9
  2.5 0.0 copy-start.10
  2.5 0.0 copy-start.11
  2.5 0.0 copy-start.12
  2.6 0.0 copy-start.13
  2.6 0.0 copy-done.14
  2.6 0.0 copy-done
  2.6 18.6 %shard_map.158.ghost_ref = bf16[5120,128]{1,0:T(8,128)(2,1)S(1)} custom-call(s32[1,10,512]{2,1,0:T(8,128)S(1)} %copy.17.rows_ref, bf16[4096,128]{1,0:T(8,128)(2,1)S(1)} %bitcast.17), custom_call_target="tpu_custom_call" | custom-call | tf_op jit(solution)/shard_map/pallas_call | solution.py:443
  21.4 78.7 %shard_map.159 = (bf16[4096,128]{1,0:T(8,128)(2,1)}, bf16[1024,128]{1,0:T(8,128)(2,1)S(1)}) custom-call(s32[1]{0:T(128)} %bitcast.brick_ref, f32[1,3,65536]{2,1,0:T(4,128)S(1)} %copy.18.geom_ref, s32[1,65536]{1,0:T(1,128)S(1)} %copy-done.2, bf16[4096,128]{1,0:T(8,128)(2,1)S(1)} %bitcast.18, bf16[5120,128]{1,0:T(8,128)(2,1)S(1)} %shard_map.158.ghost_ref, ...), custom_call_target="tpu_custom_call" | custom-call | flops 8999999488 | bytes 6000000 | tf_op jit(solution)/shard_map/pallas_call | solution.py:302
  100.1 0.0 copy-start.1
  100.1 0.7 copy-done.1
  100.8 8.2 %shard_map.160 = bf16[8,128,128]{2,1,0:T(8,128)(2,1)} custom-call(bf16[8,128,128]{2,1,0:T(8,128)(2,1)} %bitcast.19), custom_call_target="tpu_custom_call" | custom-call | tf_op jit(solution)/shard_map/pallas_call | solution.py:499
  109.1 0.1 stack.35
  109.2 1.7 %select_bitcast_fusion = bf16[1,8,128,128]{3,2,1,0:T(8,128)(2,1)} fusion(bf16[8,128,128]{2,1,0:T(8,128)(2,1)} %shard_map.160, pred[8]{0:T(512)(128)(4,1)S(1)} %stack.35), kind=kLoop, calls=%fused_computation | loop fusion | flops 131072 | bytes 524296 | tf_op jit(solution)/shard_map/broadcast_in_dim | solution.py:546
  (13 shorter events, 0.0 us)
Async XLA Ops:
  0.6 2.0 %copy-start = (bf16[1,4096,128]{2,1,0:T(8,128)(2,1)S(1)}, bf16[1,4096,128]{2,1,0:T(8,128)(2,1)}, u32[]{:S(2)}) copy-start(bf16[1,4096,128]{2,1,0:T(8,128)(2,1)} %param.15) | copy-start | bytes 3145732
  0.6 1.9 %copy-start.14 = (s32[1,10,512]{2,0,1:T(1,128)S(1)}, s32[1,10,512]{2,0,1:T(1,128)}, u32[]{:S(2)}) copy-start(s32[1,10,512]{2,0,1:T(1,128)} %param.19) | copy-start | bytes 61444
  2.4 18.8 %copy-start.2 = (s32[1,65536]{1,0:T(1,128)S(1)}, s32[1,65536]{1,0:T(1,128)}, u32[]{:S(2)}) copy-start(s32[1,65536]{1,0:T(1,128)} %recv_ref.1) | copy-start | bytes 786436
  2.4 18.8 %copy-start.3 = (s32[1,65536]{1,0:T(1,128)S(1)}, s32[1,65536]{1,0:T(1,128)}, u32[]{:S(2)}) copy-start(s32[1,65536]{1,0:T(1,128)} %send_hbm.1) | copy-start | bytes 786436
  2.4 18.8 %copy-start.4 = (bf16[3,128,128]{2,1,0:T(8,128)(2,1)S(1)}, bf16[3,128,128]{2,1,0:T(8,128)(2,1)}, u32[]{:S(2)}) copy-start(bf16[3,128,128]{2,1,0:T(8,128)(2,1)} %pe_w1_ref.1) | copy-start | bytes 294916
  2.5 18.8 %copy-start.5 = (bf16[2,128,128]{2,1,0:T(8,128)(2,1)S(1)}, bf16[2,128,128]{2,1,0:T(8,128)(2,1)}, u32[]{:S(2)}) copy-start(bf16[2,128,128]{2,1,0:T(8,128)(2,1)} %pn_w1_ref.1) | copy-start | bytes 196612
  2.5 18.8 %copy-start.6 = (bf16[128,128]{1,0:T(8,128)(2,1)S(1)}, bf16[128,128]{1,0:T(8,128)(2,1)}, u32[]{:S(2)}) copy-start(bf16[128,128]{1,0:T(8,128)(2,1)} %enc_w2_ref.1) | copy-start | bytes 98308
  2.5 18.8 %copy-start.7 = (bf16[128,128]{1,0:T(8,128)(2,1)S(1)}, bf16[128,128]{1,0:T(8,128)(2,1)}, u32[]{:S(2)}) copy-start(bf16[128,128]{1,0:T(8,128)(2,1)} %pe_w2_ref.1) | copy-start | bytes 98308
  2.5 18.8 %copy-start.8 = (bf16[128,128]{1,0:T(8,128)(2,1)S(1)}, bf16[128,128]{1,0:T(8,128)(2,1)}, u32[]{:S(2)}) copy-start(bf16[128,128]{1,0:T(8,128)(2,1)} %pn_w2_ref.1) | copy-start | bytes 98308
  2.5 18.8 %copy-start.9 = (s32[1,4096]{1,0:T(1,128)S(1)}, s32[1,4096]{1,0:T(1,128)}, u32[]{:S(2)}) copy-start(s32[1,4096]{1,0:T(1,128)} %dest_ref.1) | copy-start | bytes 49156
  2.5 18.8 %copy-start.10 = (f32[4,128]{1,0:T(4,128)S(1)}, f32[4,128]{1,0:T(4,128)}, u32[]{:S(2)}) copy-start(f32[4,128]{1,0:T(4,128)} %enc_w1_ref.1) | copy-start | bytes 6148
  2.5 18.8 %copy-start.11 = (f32[128]{0:T(128)S(1)}, f32[128]{0:T(128)}, u32[]{:S(2)}) copy-start(f32[128]{0:T(128)} %param.22) | copy-start | bytes 1540
  2.5 18.8 %copy-start.12 = (f32[128]{0:T(128)S(1)}, f32[128]{0:T(128)}, u32[]{:S(2)}) copy-start(f32[128]{0:T(128)} %param.26) | copy-start | bytes 1540
  2.6 18.8 %copy-start.13 = (f32[128]{0:T(128)S(1)}, f32[128]{0:T(128)}, u32[]{:S(2)}) copy-start(f32[128]{0:T(128)} %param.29) | copy-start | bytes 1540
  100.1 0.7 copy-start.1

commit v5 on v4

--- a/solution.py
+++ b/solution.py
@@ -81,8 +81,7 @@
             send_hbm.at[:, pl.ds(pl.multiple_of(at, CHUNK), CHUNK)], slots[slot], sems.at[slot]
         )
 
-    for ahead in (-2, -1, 0):
-        fetch(ahead % 4, ahead).start()
+    fetch(0, 0).start()
 
     w_first[...] = jnp.zeros_like(w_first)
     w_enc[...] = jnp.zeros_like(w_enc)
@@ -192,7 +191,8 @@
 
     def messages():
         out = dot(mixed[...], w_msg[...])
-        message[...] = normed_pair(out)
+        message[:, 0:128] = normed(out[:, 0:128])
+        message[:, 128:256] = normed(out[:, 128:256])
 
     def gather_up(tile, q, first):
         out = None
@@ -207,19 +207,20 @@
         else:
             summed[pl.ds(at, TILE), :] += out
 
-    def body(t, q, final=False):
+    def body(t, q, final=False, initial=False):
         chunk = t * 4 + q
 
         def tile(back):
             at = t * (4 // PER) + (q - back) // PER
-            return at if final else jnp.maximum(at, 0)
-
-        live = lambda back: not final or q < back
+            return at
+
+        live = lambda back: (not final or q < back) and (not initial or q >= back)
         if live(2):
             fetch((q - 2) % 4, chunk - 2).wait()
-        if live(-1):
+        if not final:
             fetch((q + 1) % 4, chunk + 1).start()
-        gather_up(tile(4), q, q % PER == 0)
+        if not initial:
+            gather_up(tile(4), q, q % PER == 0)
         if live(3):
             messages()
         if live(2):
@@ -229,13 +230,16 @@
         if live(0):
             first_layer(chunk, tile(0), q)
 
-    @pl.loop(0, chunks // 4)
+    for q in range(4):
+        body(0, q, initial=True)
+
+    @pl.loop(1, chunks // 4)
     def _(t):
         for q in range(4):
             body(t, q)
 
     for q in range(4):
-        body(chunks // 4, q, True)
+        body(chunks // 4, q, final=True)
     fetch(0, chunks).wait()
 
     brick = brick_ref[0]

time: 111 us -> 107 us (0.964)
  Pallas kernels: 106 us -> 102 us
    pallas_call x1, Pallas kernels: 78.7 us -> 74.6 us  [edge_call(): pl.pallas_call(edge_kernel, in_specs=[pl.BlockSpec(memory_space=pltpu.SME...]
where the time goes in v5:
time: 107 us
  Pallas kernels  102 us (95%)
  local copies, waits for them, and re-layouts  2.66 us (2%)
  other arithmetic  1.74 us (2%)
    pallas_call x1, Pallas kernels, edge_call(): pl.pallas_call(edge_kernel, in_specs=[pl.BlockSpec(memory_space=pltpu.SME...  74.6 us
    pallas_call x1, Pallas kernels, ghost_call(): pl.pallas_call(ghost_kernel, in_specs=[pl.BlockSpec(memory_space=pltpu.SM...  18.6 us
    pallas_call x1, Pallas kernels, migrant_call(): pl.pallas_call(migrant_kernel, in_specs=[pl.BlockSpec(memory_space=pltpu....  8.34 us
    unnamed x32, local copies, waits for them, and re-layouts  2.55 us

profile of v5, /device:TPU:1, one launch (start us, length us, event | category | flops | bytes accessed | tf_op | source)
XLA Modules:
  0.0 107.0 jit_solution(14778212217162655351)
XLA Ops:
  0.6 0.0 copy-start
  0.6 0.0 copy-start.14
  0.7 1.8 %copy.18.geom_ref = f32[1,3,65536]{2,1,0:T(4,128)S(1)} copy(f32[1,3,65536]{2,0,1:T(1,128)} %param.16) | data formatting | bytes 1572864 | tf_op args[1]
  2.4 0.0 copy-start.2
  2.4 0.0 copy-start.3
  2.4 0.0 copy-start.4
  2.5 0.0 copy-start.5
  2.5 0.0 copy-start.6
  2.5 0.0 copy-start.7
  2.5 0.0 copy-start.8
  2.5 0.0 copy-start.9
  2.5 0.0 copy-start.10
  2.5 0.0 copy-start.11
  2.5 0.0 copy-start.12
  2.6 0.0 copy-start.13
  2.6 0.0 copy-done.14
  2.6 0.0 copy-done
  2.6 18.6 %shard_map.158.ghost_ref = bf16[5120,128]{1,0:T(8,128)(2,1)S(1)} custom-call(s32[1,10,512]{2,1,0:T(8,128)S(1)} %copy.17.rows_ref, bf16[4096,128]{1,0:T(8,128)(2,1)S(1)} %bitcast.17), custom_call_target="tpu_custom_call" | custom-call | tf_op jit(solution)/shard_map/pallas_call | solution.py:447
  21.4 74.6 %shard_map.159 = (bf16[4096,128]{1,0:T(8,128)(2,1)}, bf16[1024,128]{1,0:T(8,128)(2,1)S(1)}) custom-call(s32[1]{0:T(128)} %bitcast.brick_ref, f32[1,3,65536]{2,1,0:T(4,128)S(1)} %copy.18.geom_ref, s32[1,65536]{1,0:T(1,128)S(1)} %copy-done.2, bf16[4096,128]{1,0:T(8,128)(2,1)S(1)} %bitcast.18, bf16[5120,128]{1,0:T(8,128)(2,1)S(1)} %shard_map.158.ghost_ref, ...), custom_call_target="tpu_custom_call" | custom-call | flops 8999999488 | bytes 6000000 | tf_op jit(solution)/shard_map/pallas_call | solution.py:306
  96.0 0.0 copy-start.1
  96.0 0.7 copy-done.1
  96.7 8.3 %shard_map.160 = bf16[8,128,128]{2,1,0:T(8,128)(2,1)} custom-call(bf16[8,128,128]{2,1,0:T(8,128)(2,1)} %bitcast.19), custom_call_target="tpu_custom_call" | custom-call | tf_op jit(solution)/shard_map/pallas_call | solution.py:503
  105.1 0.1 stack.35
  105.3 1.7 %select_bitcast_fusion = bf16[1,8,128,128]{3,2,1,0:T(8,128)(2,1)} fusion(bf16[8,128,128]{2,1,0:T(8,128)(2,1)} %shard_map.160, pred[8]{0:T(512)(128)(4,1)S(1)} %stack.35), kind=kLoop, calls=%fused_computation | loop fusion | flops 131072 | bytes 524296 | tf_op jit(solution)/shard_map/broadcast_in_dim | solution.py:550
  (13 shorter events, 0.0 us)
Async XLA Ops:
  0.6 2.0 %copy-start = (bf16[1,4096,128]{2,1,0:T(8,128)(2,1)S(1)}, bf16[1,4096,128]{2,1,0:T(8,128)(2,1)}, u32[]{:S(2)}) copy-start(bf16[1,4096,128]{2,1,0:T(8,128)(2,1)} %param.15) | copy-start | bytes 3145732
  0.6 1.9 %copy-start.14 = (s32[1,10,512]{2,0,1:T(1,128)S(1)}, s32[1,10,512]{2,0,1:T(1,128)}, u32[]{:S(2)}) copy-start(s32[1,10,512]{2,0,1:T(1,128)} %param.19) | copy-start | bytes 61444
  2.4 18.8 %copy-start.2 = (s32[1,65536]{1,0:T(1,128)S(1)}, s32[1,65536]{1,0:T(1,128)}, u32[]{:S(2)}) copy-start(s32[1,65536]{1,0:T(1,128)} %recv_ref.1) | copy-start | bytes 786436
  2.4 18.8 %copy-start.3 = (s32[1,65536]{1,0:T(1,128)S(1)}, s32[1,65536]{1,0:T(1,128)}, u32[]{:S(2)}) copy-start(s32[1,65536]{1,0:T(1,128)} %send_hbm.1) | copy-start | bytes 786436
  2.4 18.8 %copy-start.4 = (bf16[3,128,128]{2,1,0:T(8,128)(2,1)S(1)}, bf16[3,128,128]{2,1,0:T(8,128)(2,1)}, u32[]{:S(2)}) copy-start(bf16[3,128,128]{2,1,0:T(8,128)(2,1)} %pe_w1_ref.1) | copy-start | bytes 294916
  2.5 18.8 %copy-start.5 = (bf16[2,128,128]{2,1,0:T(8,128)(2,1)S(1)}, bf16[2,128,128]{2,1,0:T(8,128)(2,1)}, u32[]{:S(2)}) copy-start(bf16[2,128,128]{2,1,0:T(8,128)(2,1)} %pn_w1_ref.1) | copy-start | bytes 196612
  2.5 18.8 %copy-start.6 = (bf16[128,128]{1,0:T(8,128)(2,1)S(1)}, bf16[128,128]{1,0:T(8,128)(2,1)}, u32[]{:S(2)}) copy-start(bf16[128,128]{1,0:T(8,128)(2,1)} %enc_w2_ref.1) | copy-start | bytes 98308
  2.5 18.8 %copy-start.7 = (bf16[128,128]{1,0:T(8,128)(2,1)S(1)}, bf16[128,128]{1,0:T(8,128)(2,1)}, u32[]{:S(2)}) copy-start(bf16[128,128]{1,0:T(8,128)(2,1)} %pe_w2_ref.1) | copy-start | bytes 98308
  2.5 18.8 %copy-start.8 = (bf16[128,128]{1,0:T(8,128)(2,1)S(1)}, bf16[128,128]{1,0:T(8,128)(2,1)}, u32[]{:S(2)}) copy-start(bf16[128,128]{1,0:T(8,128)(2,1)} %pn_w2_ref.1) | copy-start | bytes 98308
  2.5 18.8 %copy-start.9 = (s32[1,4096]{1,0:T(1,128)S(1)}, s32[1,4096]{1,0:T(1,128)}, u32[]{:S(2)}) copy-start(s32[1,4096]{1,0:T(1,128)} %dest_ref.1) | copy-start | bytes 49156
  2.5 18.8 %copy-start.10 = (f32[4,128]{1,0:T(4,128)S(1)}, f32[4,128]{1,0:T(4,128)}, u32[]{:S(2)}) copy-start(f32[4,128]{1,0:T(4,128)} %enc_w1_ref.1) | copy-start | bytes 6148
  2.5 18.8 %copy-start.11 = (f32[128]{0:T(128)S(1)}, f32[128]{0:T(128)}, u32[]{:S(2)}) copy-start(f32[128]{0:T(128)} %param.22) | copy-start | bytes 1540
  2.5 18.8 %copy-start.12 = (f32[128]{0:T(128)S(1)}, f32[128]{0:T(128)}, u32[]{:S(2)}) copy-start(f32[128]{0:T(128)} %param.26) | copy-start | bytes 1540
  2.6 18.8 %copy-start.13 = (f32[128]{0:T(128)S(1)}, f32[128]{0:T(128)}, u32[]{:S(2)}) copy-start(f32[128]{0:T(128)} %param.29) | copy-start | bytes 1540
  96.0 0.7 copy-start.1

commit v6 on v5

--- a/solution.py
+++ b/solution.py
@@ -12,7 +12,7 @@
 CHUNK = 1024
 PAIR = 512
 PER = 2048 // CHUNK
-BLOCK = 1024
+BLOCK = 2048
 PARTS = 4096
 GHOST = 5120
 STEP_ROW = (-1, -1, -1, 0, 0, 1, 1, 1)

time: 107 us -> 106 us (level)
  Pallas kernels: 102 us -> 100 us
    pallas_call x1, Pallas kernels: 74.6 us -> 73.1 us  [edge_call(): pl.pallas_call(edge_kernel, in_specs=[pl.BlockSpec(memory_space=pltpu.SME...]
where the time goes in v6:
time: 106 us; the launch traced here: 105 us
  Pallas kernels  100 us (94%)
  local copies, waits for them, and re-layouts  2.66 us (3%)
  other arithmetic  1.74 us (2%)
    pallas_call x1, Pallas kernels, edge_call(): pl.pallas_call(edge_kernel, in_specs=[pl.BlockSpec(memory_space=pltpu.SME...  73.1 us
    pallas_call x1, Pallas kernels, ghost_call(): pl.pallas_call(ghost_kernel, in_specs=[pl.BlockSpec(memory_space=pltpu.SM...  18.6 us
    pallas_call x1, Pallas kernels, migrant_call(): pl.pallas_call(migrant_kernel, in_specs=[pl.BlockSpec(memory_space=pltpu....  8.25 us
    unnamed x32, local copies, waits for them, and re-layouts  2.55 us

profile of v6, /device:TPU:1, one launch (start us, length us, event | category | flops | bytes accessed | tf_op | source)
XLA Modules:
  0.0 105.4 jit_solution(7185452530585436920)
XLA Ops:
  0.7 1.8 %copy.18.geom_ref = f32[1,3,65536]{2,1,0:T(4,128)S(1)} copy(f32[1,3,65536]{2,0,1:T(1,128)} %param.16) | data formatting | bytes 1572864 | tf_op args[1]
  2.4 0.0 copy-start.2
  2.4 0.0 copy-start.3
  2.4 0.0 copy-start.4
  2.5 0.0 copy-start.5
  2.5 0.0 copy-start.6
  2.5 0.0 copy-start.7
  2.5 0.0 copy-start.8
  2.5 0.0 copy-start.9
  2.5 0.0 copy-start.10
  2.5 0.0 copy-start.11
  2.5 0.0 copy-start.12
  2.6 0.0 copy-start.13
  2.6 0.0 copy-done.14
  2.6 18.6 %shard_map.158.ghost_ref = bf16[5120,128]{1,0:T(8,128)(2,1)S(1)} custom-call(s32[1,10,512]{2,1,0:T(8,128)S(1)} %copy.17.rows_ref, bf16[4096,128]{1,0:T(8,128)(2,1)S(1)} %bitcast.17), custom_call_target="tpu_custom_call" | custom-call | tf_op jit(solution)/shard_map/pallas_call | solution.py:447
  21.3 0.0 copy-done.2
  21.3 0.0 copy-done.3
  21.3 0.0 copy-done.4
  21.4 73.1 %shard_map.159 = (bf16[4096,128]{1,0:T(8,128)(2,1)}, bf16[1024,128]{1,0:T(8,128)(2,1)S(1)}) custom-call(s32[1]{0:T(128)} %bitcast.brick_ref, f32[1,3,65536]{2,1,0:T(4,128)S(1)} %copy.18.geom_ref, s32[1,65536]{1,0:T(1,128)S(1)} %copy-done.2, bf16[4096,128]{1,0:T(8,128)(2,1)S(1)} %bitcast.18, bf16[5120,128]{1,0:T(8,128)(2,1)S(1)} %shard_map.158.ghost_ref, ...), custom_call_target="tpu_custom_call" | custom-call | flops 8999999488 | bytes 6000000 | tf_op jit(solution)/shard_map/pallas_call | solution.py:306
  94.5 0.0 copy-start.1
  94.5 0.7 copy-done.1
  95.2 8.2 %shard_map.160 = bf16[8,128,128]{2,1,0:T(8,128)(2,1)} custom-call(bf16[8,128,128]{2,1,0:T(8,128)(2,1)} %bitcast.19), custom_call_target="tpu_custom_call" | custom-call | tf_op jit(solution)/shard_map/pallas_call | solution.py:503
  103.5 0.1 stack.35
  103.6 1.7 %select_bitcast_fusion = bf16[1,8,128,128]{3,2,1,0:T(8,128)(2,1)} fusion(bf16[8,128,128]{2,1,0:T(8,128)(2,1)} %shard_map.160, pred[8]{0:T(512)(128)(4,1)S(1)} %stack.35), kind=kLoop, calls=%fused_computation | loop fusion | flops 131072 | bytes 524296 | tf_op jit(solution)/shard_map/broadcast_in_dim | solution.py:550
  (13 shorter events, 0.0 us)
Async XLA Ops:
  0.6 2.0 %copy-start = (bf16[1,4096,128]{2,1,0:T(8,128)(2,1)S(1)}, bf16[1,4096,128]{2,1,0:T(8,128)(2,1)}, u32[]{:S(2)}) copy-start(bf16[1,4096,128]{2,1,0:T(8,128)(2,1)} %param.15) | copy-start | bytes 3145732
  0.6 1.9 %copy-start.14 = (s32[1,10,512]{2,0,1:T(1,128)S(1)}, s32[1,10,512]{2,0,1:T(1,128)}, u32[]{:S(2)}) copy-start(s32[1,10,512]{2,0,1:T(1,128)} %param.19) | copy-start | bytes 61444
  2.4 18.8 %copy-start.2 = (s32[1,65536]{1,0:T(1,128)S(1)}, s32[1,65536]{1,0:T(1,128)}, u32[]{:S(2)}) copy-start(s32[1,65536]{1,0:T(1,128)} %recv_ref.1) | copy-start | bytes 786436
  2.4 18.8 %copy-start.3 = (s32[1,65536]{1,0:T(1,128)S(1)}, s32[1,65536]{1,0:T(1,128)}, u32[]{:S(2)}) copy-start(s32[1,65536]{1,0:T(1,128)} %send_hbm.1) | copy-start | bytes 786436
  2.4 18.8 %copy-start.4 = (bf16[3,128,128]{2,1,0:T(8,128)(2,1)S(1)}, bf16[3,128,128]{2,1,0:T(8,128)(2,1)}, u32[]{:S(2)}) copy-start(bf16[3,128,128]{2,1,0:T(8,128)(2,1)} %pe_w1_ref.1) | copy-start | bytes 294916
  2.5 18.8 %copy-start.5 = (bf16[2,128,128]{2,1,0:T(8,128)(2,1)S(1)}, bf16[2,128,128]{2,1,0:T(8,128)(2,1)}, u32[]{:S(2)}) copy-start(bf16[2,128,128]{2,1,0:T(8,128)(2,1)} %pn_w1_ref.1) | copy-start | bytes 196612
  2.5 18.8 %copy-start.6 = (bf16[128,128]{1,0:T(8,128)(2,1)S(1)}, bf16[128,128]{1,0:T(8,128)(2,1)}, u32[]{:S(2)}) copy-start(bf16[128,128]{1,0:T(8,128)(2,1)} %enc_w2_ref.1) | copy-start | bytes 98308
  2.5 18.8 %copy-start.7 = (bf16[128,128]{1,0:T(8,128)(2,1)S(1)}, bf16[128,128]{1,0:T(8,128)(2,1)}, u32[]{:S(2)}) copy-start(bf16[128,128]{1,0:T(8,128)(2,1)} %pe_w2_ref.1) | copy-start | bytes 98308
  2.5 18.8 %copy-start.8 = (bf16[128,128]{1,0:T(8,128)(2,1)S(1)}, bf16[128,128]{1,0:T(8,128)(2,1)}, u32[]{:S(2)}) copy-start(bf16[128,128]{1,0:T(8,128)(2,1)} %pn_w2_ref.1) | copy-start | bytes 98308
  2.5 18.8 %copy-start.9 = (s32[1,4096]{1,0:T(1,128)S(1)}, s32[1,4096]{1,0:T(1,128)}, u32[]{:S(2)}) copy-start(s32[1,4096]{1,0:T(1,128)} %dest_ref.1) | copy-start | bytes 49156
  2.5 18.8 %copy-start.10 = (f32[4,128]{1,0:T(4,128)S(1)}, f32[4,128]{1,0:T(4,128)}, u32[]{:S(2)}) copy-start(f32[4,128]{1,0:T(4,128)} %enc_w1_ref.1) | copy-start | bytes 6148
  2.5 18.8 %copy-start.11 = (f32[128]{0:T(128)S(1)}, f32[128]{0:T(128)}, u32[]{:S(2)}) copy-start(f32[128]{0:T(128)} %param.22) | copy-start | bytes 1540
  2.5 18.8 %copy-start.12 = (f32[128]{0:T(128)S(1)}, f32[128]{0:T(128)}, u32[]{:S(2)}) copy-start(f32[128]{0:T(128)} %param.26) | copy-start | bytes 1540
  2.6 18.8 %copy-start.13 = (f32[128]{0:T(128)S(1)}, f32[128]{0:T(128)}, u32[]{:S(2)}) copy-start(f32[128]{0:T(128)} %param.29) | copy-start | bytes 1540
  94.5 0.7 copy-start.1
